TPU v7x, 512 devices: a whole 4x8x8 slice. The times are simulated.
512 devices in a mesh: lat: 8 (over x, z_lo), lon: 64 (over y, z_hi, core).
Axes of the slice: x: 4, y: 8, z: 8 (z_hi: 4, z_lo: 2; z = z_hi * 2 + z_lo), core: 2. Of those that a mesh axis runs over, the one named last changes fastest.
Arguments:
- fields: bfloat16 [4, 96, 768, 192], P(None, 'lat', 'lon'), may hold values from -6 to 6
- region_one: int32 [4, 96, 768], P(None, 'lat', 'lon'), may hold values from 0 to 3
- region_two: int32 [4, 48, 384], P(None, 'lat', 'lon'), may hold values from 0 to 3
- valid_rows: int32 [96], replicated, may hold values 0 or 1
- gain_one: float32 [192], replicated, may hold values from 0.1 to 1.9
- project_one: bfloat16 [192, 576], replicated, may hold values from -0.4375 to 0.4375
- output_one: bfloat16 [192, 192], replicated, may hold values from -0.4375 to 0.4375
- table_one: bfloat16 [16, 2, 6, 3312], P('lat'), may hold values from -4 to 305
- gain_two: float32 [192], replicated, may hold values from 0.1 to 1.9
- up_weight: bfloat16 [192, 768], replicated, may hold values from -0.4375 to 0.4375
- down_weight: bfloat16 [768, 192], replicated, may hold values from -0.21875 to 0.21875
- gain_three: float32 [768], replicated, may hold values from 0.1 to 1.9
- merge_weight: bfloat16 [768, 384], replicated, may hold values from -0.21875 to 0.21875
- gain_four: float32 [384], replicated, may hold values from 0.1 to 1.9
- project_two: bfloat16 [384, 1152], replicated, may hold values from -0.3125 to 0.3125
- output_two: bfloat16 [384, 384], replicated, may hold values from -0.3125 to 0.3125
- table_two: bfloat16 [8, 2, 12, 3312], P('lat'), may hold values from -4 to 305
Outputs:
- refined: bfloat16 [4, 48, 384, 384], P(None, 'lat', 'lon')
All inputs are finite; a program needn't handle non-finite values.
Results may differ from a plain program's by a relative error of at most 0.019.
Values may be sent and summed in bfloat16 or wider, within the bound.
A program may use at most 64 MiB of HBM per device.

v0:
```python
import jax
import jax.numpy as jnp
import numpy as np
from jax import lax
from jax.sharding import PartitionSpec as P

H1 = 6
H2 = 12
WZ = 2
WLAT = 6
WLON = 12


def from_behind(block, axis, distance):
    devices = range(lax.axis_size(axis))
    route = [((i - distance) % len(devices), i) for i in devices]
    return lax.ppermute(block, axis, route)


def partner(block, axis, stride):
    count = lax.axis_size(axis)
    route = []
    for low in range(count):
        high = low | 1 << stride
        if high != low and high < count:
            route += [(low, high), (high, low)]
    return lax.ppermute(block, axis, route)


def position_index():
    window_size = WZ * WLAT * WLON
    places = np.arange(window_size)
    level_pos = places // (WLAT * WLON)
    band_pos = places // WLON % WLAT
    sector = places % WLON
    pair_index = (
        (
            (level_pos[:, None] * WZ + level_pos[None, :]) * (WLAT * WLAT)
            + band_pos[:, None] * WLAT
            + band_pos[None, :]
        )
        * (2 * WLON - 1)
        + sector[:, None]
        - sector[None, :]
        + WLON
        - 1
    )
    return pair_index.astype(np.int32)


def to_windows(field):
    levels, lat_rows, lon_cols, feature_width = field.shape
    split = field.reshape(
        levels // WZ, WZ, lat_rows // WLAT, WLAT, lon_cols // WLON, WLON, feature_width
    )
    return split.transpose(2, 0, 4, 1, 3, 5, 6).reshape(
        lat_rows // WLAT, levels // WZ, lon_cols // WLON, WZ * WLAT * WLON, feature_width
    )


def from_windows(windows, levels, lat_rows, lon_cols):
    feature_width = windows.shape[-1]
    split = windows.reshape(
        lat_rows // WLAT, levels // WZ, lon_cols // WLON, WZ, WLAT, WLON, feature_width
    )
    return split.transpose(1, 3, 0, 4, 2, 5, 6).reshape(levels, lat_rows, lon_cols, feature_width)


def normalize(field, gain_vec):
    values = field.astype(jnp.float32)
    center = jnp.mean(values, -1, keepdims=True)
    spread = jnp.mean((values - center) ** 2, -1, keepdims=True)
    return (values - center) * lax.rsqrt(spread + 1e-05) * gain_vec


def advance(field):
    upper_rows = from_behind(field[:, : WLAT // 2], "lat", -1)
    field = jnp.concatenate([field[:, WLAT // 2 :], upper_rows], axis=1)
    right_cols = from_behind(field[:, :, : WLON // 2], "lon", -1)
    return jnp.concatenate([field[:, :, WLON // 2 :], right_cols], axis=2)


def retreat(field):
    left_cols = from_behind(field[:, :, -(WLON // 2) :], "lon", 1)
    field = jnp.concatenate([left_cols, field[:, :, : -(WLON // 2)]], axis=2)
    lower_rows = from_behind(field[:, -(WLAT // 2) :], "lat", 1)
    field = jnp.concatenate([lower_rows, field[:, : -(WLAT // 2)]], axis=1)
    return jnp.roll(field, WZ // 2, 0)


def window_attention(normed, project, output, bias_table, region, key_valid, head_count):
    levels, lat_rows, lon_cols, feature_width = normed.shape
    head_size = feature_width // head_count
    window_size = WZ * WLAT * WLON
    index_table = position_index()
    eye_mask = jnp.eye(window_size, dtype=bool)
    windows = to_windows(normed)
    region_win = to_windows(region[..., None])[..., 0]
    valid_full = jnp.broadcast_to(key_valid[None, :, None, None], (levels, lat_rows, lon_cols, 1))
    valid_win = to_windows(valid_full)[..., 0]

    def one_band(operands):
        tokens_win, table_win, region_band, valid_band = operands
        level_count = tokens_win.shape[0]
        sector_count = tokens_win.shape[1]
        flat = tokens_win.reshape(-1, feature_width)
        mixed = jnp.dot(flat, project, preferred_element_type=jnp.float32).astype(jnp.bfloat16)
        mixed = mixed.reshape(level_count, sector_count, window_size, 3, head_count, head_size)
        queries = mixed[:, :, :, 0]
        key_vecs = mixed[:, :, :, 1]
        value_vecs = mixed[:, :, :, 2]
        scores = jnp.einsum(
            "zwqhd,zwkhd->zwhqk", queries, key_vecs, preferred_element_type=jnp.float32
        ) * head_size ** (-0.5)
        bias = jnp.take(table_win, index_table, axis=2).astype(jnp.float32)
        scores = scores + bias[:, None]
        allowed = (region_band[..., :, None] == region_band[..., None, :]) & (
            (valid_band[..., None, :] == 1) | eye_mask
        )
        allowed = allowed[:, :, None]
        top_score = jnp.max(jnp.where(allowed, scores, -jnp.inf), -1, keepdims=True)
        weights = jnp.where(allowed, jnp.exp(scores - top_score), 0.0)
        probs = (weights / jnp.sum(weights, -1, keepdims=True)).astype(jnp.bfloat16)
        heads_out = jnp.einsum(
            "zwhqk,zwkhd->zwqhd", probs, value_vecs, preferred_element_type=jnp.float32
        ).astype(jnp.bfloat16)
        heads_out = heads_out.reshape(-1, feature_width)
        projected = jnp.dot(heads_out, output, preferred_element_type=jnp.float32).astype(
            jnp.bfloat16
        )
        return projected.reshape(level_count, sector_count, window_size, feature_width)

    result = lax.map(one_band, (windows, bias_table, region_win, valid_win))
    return from_windows(result, levels, lat_rows, lon_cols)


def coarse_attention(normed, project, output, bias_table, region, key_valid, head_count):
    own_cols = normed.shape[2]
    partner_tokens, partner_region = partner((normed, region.astype(jnp.bfloat16)), "lon", 0)
    partner_region = partner_region.astype(jnp.int32)
    is_odd = lax.axis_index("lon") % 2
    tokens_pair = jnp.where(
        is_odd == 1,
        jnp.concatenate([partner_tokens, normed], axis=2),
        jnp.concatenate([normed, partner_tokens], axis=2),
    )
    region_pair = jnp.where(
        is_odd == 1,
        jnp.concatenate([partner_region, region], axis=2),
        jnp.concatenate([region, partner_region], axis=2),
    )
    result = window_attention(
        tokens_pair, project, output, bias_table, region_pair, key_valid, head_count
    )
    return lax.dynamic_slice_in_dim(result, is_odd * own_cols, own_cols, 2)


def feed_forward(state, gain_vec, up_weight, down_weight):
    feature_width = state.shape[-1]
    normed = normalize(state, gain_vec).astype(jnp.bfloat16).reshape(-1, feature_width)
    inner = jax.nn.gelu(
        jnp.dot(normed, up_weight, preferred_element_type=jnp.float32), approximate=False
    ).astype(jnp.bfloat16)
    grown = jnp.dot(inner, down_weight, preferred_element_type=jnp.float32).reshape(state.shape)
    return (state.astype(jnp.float32) + grown).astype(jnp.bfloat16)


def merge_patches(field, gain_vec, merge_weight):
    levels, lat_rows, lon_cols, feature_width = field.shape
    patches = field.reshape(levels, lat_rows // 2, 2, lon_cols // 2, 2, feature_width)
    patches = patches.transpose(0, 1, 3, 2, 4, 5).reshape(
        levels, lat_rows // 2, lon_cols // 2, 4 * feature_width
    )
    normed = normalize(patches, gain_vec).astype(jnp.bfloat16).reshape(-1, 4 * feature_width)
    coarse = jnp.dot(normed, merge_weight, preferred_element_type=jnp.float32).astype(jnp.bfloat16)
    return coarse.reshape(levels, lat_rows // 2, lon_cols // 2, merge_weight.shape[1])


def add_round(first_term, second_term):
    return (first_term.astype(jnp.float32) + second_term.astype(jnp.float32)).astype(jnp.bfloat16)


def shards(
    fields,
    region_one,
    region_two,
    valid_rows,
    gain_one,
    project_one,
    output_one,
    table_one,
    gain_two,
    up_weight,
    down_weight,
    gain_three,
    merge_weight,
    gain_four,
    project_two,
    output_two,
    table_two,
):
    lat_rows = fields.shape[1]
    band_start = lax.axis_index("lat") * lat_rows
    keep_one = lax.dynamic_slice_in_dim(jnp.roll(valid_rows, -(WLAT // 2)), band_start, lat_rows)
    coarse_valid = jnp.maximum(valid_rows[0::2], valid_rows[1::2])
    keep_two = lax.dynamic_slice_in_dim(
        jnp.roll(coarse_valid, -(WLAT // 2)), band_start // 2, lat_rows // 2
    )
    rolled = advance(jnp.roll(fields, -(WZ // 2), 0))
    normed_one = normalize(rolled, gain_one).astype(jnp.bfloat16)
    attended_one = window_attention(
        normed_one, project_one, output_one, table_one, region_one, keep_one, H1
    )
    state = add_round(fields, retreat(attended_one))
    block_out = feed_forward(state, gain_two, up_weight, down_weight)
    coarse = merge_patches(block_out, gain_three, merge_weight)
    rolled_two = advance(jnp.roll(coarse, -(WZ // 2), 0))
    normed_four = normalize(rolled_two, gain_four).astype(jnp.bfloat16)
    attended_two = coarse_attention(
        normed_four, project_two, output_two, table_two, region_two, keep_two, H2
    )
    return add_round(coarse, retreat(attended_two))


def solution(mesh):
    placed = (
        P(None, "lat", "lon", None),
        P(None, "lat", "lon"),
        P(None, "lat", "lon"),
        P(),
        P(),
        P(),
        P(),
        P("lat", None, None, None),
        P(),
        P(),
        P(),
        P(),
        P(),
        P(),
        P(),
        P(),
        P("lat", None, None, None),
    )
    return jax.shard_map(
        shards, mesh=mesh, in_specs=placed, out_specs=P(None, "lat", "lon", None), check_vma=False
    )
```

profile of v0, /device:TPU:32, one launch (start us, length us, event | category | flops | bytes accessed | tf_op | source)
XLA Modules:
  0.0 360.9 jit_solution(3638921524065144469)
XLA Ops:
  2.4 6.5 %collective-permute-start = (bf16[4,3,12,192]{3,0,2,1:T(4,128)(2,1)S(1)}, bf16[4,3,12,192]{3,0,2,1:T(4,128)(2,1)S(1)}, u32[]{:S(2)}, u32[]{:S(2)}) collective-permute-start(bf16[4,3,12,192]{3,0,2,1:T(4,128)(2,1)S(1)} %pad_maximum_fusion.7), channel_id=1, source_target_pairs={{64,0},{128,64},{192,128},{256,192},{320,256},{384,320},{448,384},... | collective-permute-start | bytes 165896 | tf_op jit(solution)/shard_map/ppermute | solution.py:17
  14.0 10.0 %collective-permute-start.1 = (bf16[4,12,6,192]{3,0,2,1:T(4,128)(2,1)S(1)}, bf16[4,12,6,192]{3,0,2,1:T(4,128)(2,1)S(1)}, u32[]{:S(2)}, u32[]{:S(2)}) collective-permute-start(bf16[4,12,6,192]{3,0,2,1:T(4,128)(2,1)S(1)} %get-tuple-element.205), channel_id=1, source_target_pairs={{1,0},{2,1},{3,2},{4,3},{5,4},{6,5},{7,6},{8,7},{9,8},{10,9},{11,1... | collective-permute-start | bytes 331784 | tf_op jit(solution)/shard_map/ppermute | solution.py:17
  29.4 174.2 %while.16 = (s32[]{:T(128)}, bf16[2,2,1,144,192]{4,1,3,0,2:T(2,128)(2,1)}, bf16[2,2,1,144,192]{4,1,3,0,2:T(2,128)(2,1)S(1)}, bf16[192,576]{1,0:T(8,128)(2,1)S(1)...) while((s32[]{:T(128)}, ...), condition=%wide.region_5.6_spmd.clone.clone, body=%wide.region_2.5_spmd.sunk.clone.clone.sunk | while | flops 119219376 | bytes 19901296 | solution.py:133
  30.5 2.3 copy.273
  32.8 51.3 %gather_fusion = bf16[20736,2,6]{2,1,0:T(2,128)(2,1)} fusion(bf16[2,6,3312]{1,0,2:T(2,128)(2,1)S(1)} %bitcast.122, s32[21504]{0:T(1024)S(1)} %pad_clamp_fusion.3), kind=kCustom, calls=%fused_computation.clone.clone.1 | custom fusion | bytes 1078272 | tf_op jit(solution)/shard_map/while/body/eval_jaxpr/jit(_take)/gather | solution.py:115
  84.1 21.1 %copy.274 = bf16[20736,2,6]{0,1,2:T(2,128)(2,1)S(1)} copy(bf16[20736,2,6]{2,1,0:T(2,128)(2,1)} %gather_fusion) | data formatting | bytes 995328 | tf_op jit(solution)/shard_map/while/body/eval_jaxpr/jit(_take)/gather | solution.py:115
  105.2 2.8 reshape.440
  108.0 2.1 copy.275
  117.6 2.3 copy.273
  119.9 51.3 %gather_fusion = bf16[20736,2,6]{2,1,0:T(2,128)(2,1)} fusion(bf16[2,6,3312]{1,0,2:T(2,128)(2,1)S(1)} %bitcast.122, s32[21504]{0:T(1024)S(1)} %pad_clamp_fusion.3), kind=kCustom, calls=%fused_computation.clone.clone.1 | custom fusion | bytes 1078272 | tf_op jit(solution)/shard_map/while/body/eval_jaxpr/jit(_take)/gather | solution.py:115
  171.2 21.1 %copy.274 = bf16[20736,2,6]{0,1,2:T(2,128)(2,1)S(1)} copy(bf16[20736,2,6]{2,1,0:T(2,128)(2,1)} %gather_fusion) | data formatting | bytes 995328 | tf_op jit(solution)/shard_map/while/body/eval_jaxpr/jit(_take)/gather | solution.py:115
  192.3 2.8 reshape.440
  195.1 2.1 copy.275
  205.3 1.9 collective-permute-start.2
  207.3 8.9 %collective-permute-done.2 = bf16[4,12,6,192]{3,0,2,1:T(4,128)(2,1)S(1)} collective-permute-done((bf16[4,12,6,192]{3,0,2,1:T(4,128)(2,1)S(1)}, bf16[4,12,6,192]{3,0,2,1:T(4,128)(2,1)S(1)}, u32[]{:S(2)}, u32[]{:S(2)}) %collective-permute-start.2) | collective-permute-done | bytes 110624 | tf_op jit(solution)/shard_map/ppermute | solution.py:17
  216.2 2.1 collective-permute-start.3
  218.4 6.2 %collective-permute-done.3 = bf16[4,3,12,192]{3,0,2,1:T(4,128)(2,1)S(1)} collective-permute-done((bf16[4,3,12,192]{3,0,2,1:T(4,128)(2,1)S(1)}, bf16[4,3,12,192]{3,0,2,1:T(4,128)(2,1)S(1)}, u32[]{:S(2)}, u32[]{:S(2)}) %collective-permute-start.3) | collective-permute-done | bytes 55328 | tf_op jit(solution)/shard_map/ppermute | solution.py:17
  226.7 4.3 %fusion.28 = f32[576,192]{1,0:T(8,128)S(1)} fusion(bf16[768,192]{0,1:T(8,128)(2,1)S(1)} %copy-done.20, bf16[576,192]{1,0:T(8,128)(2,1)S(1)} %reshape.379, bf16[192,768]{1,0:T(8,128)(2,1)S(1)} %copy-done.21), kind=kOutput, calls=%fused_computation.57 | convolution fusion | flops 368492544 | bytes 1253376 | tf_op jit(solution)/shard_map/dot_general | solution.py:164
  234.2 2.6 collective-permute-start.4
  236.9 2.3 copy.224
  239.2 51.3 %gather_fusion.1 = bf16[20736,2,12]{2,1,0:T(2,128)(2,1)} fusion(bf16[2,12,3312]{1,0,2:T(2,128)(2,1)S(1)} %bitcast.125, s32[21504]{0:T(1024)S(1)} %copy-done.8), kind=kCustom, calls=%fused_computation.1 | custom fusion | bytes 2073600 | tf_op jit(solution)/shard_map/while/body/eval_jaxpr/jit(_take)/gather | solution.py:115
  290.5 21.2 %copy.225 = bf16[20736,2,12]{0,1,2:T(2,128)(2,1)S(1)} copy(bf16[20736,2,12]{2,1,0:T(2,128)(2,1)} %gather_fusion.1) | data formatting | bytes 1990656 | tf_op jit(solution)/shard_map/while/body/eval_jaxpr/jit(_take)/gather | solution.py:115
  311.7 4.4 %reshape.423 = f32[144,144,2,12]{1,0,2,3:T(8,128)} reshape(bf16[20736,2,12]{0,1,2:T(2,128)(2,1)S(1)} %copy.225) | data formatting | bytes 2985984 | tf_op jit(solution)/shard_map/while/body/eval_jaxpr/convert_element_type | solution.py:115
  316.1 5.6 %copy.226 = f32[144,144,2,12]{0,1,3,2:T(8,128)} copy(f32[144,144,2,12]{1,0,2,3:T(8,128)} %reshape.423) | data formatting | bytes 3981312 | tf_op jit(solution)/shard_map/while/body/eval_jaxpr/convert_element_type | solution.py:115
  322.0 1.9 collective-permute-start.5
  324.1 2.5 collective-permute-done.5
  327.6 1.9 collective-permute-start.6
  333.4 2.7 bitcast_add_fusion.1
  338.8 2.0 collective-permute-start.8
  340.8 11.0 %collective-permute-done.8 = bf16[4,6,6,384]{3,2,1,0:T(8,128)(2,1)S(1)} collective-permute-done((bf16[4,6,6,384]{3,2,1,0:T(8,128)(2,1)S(1)}, bf16[4,6,6,384]{3,2,1,0:T(8,128)(2,1)S(1)}, u32[]{:S(2)}, u32[]{:S(2)}) %collective-permute-start.8) | collective-permute-done | bytes 110624 | tf_op jit(solution)/shard_map/ppermute | solution.py:17
  351.8 3.1 collective-permute-start.9
  355.0 5.2 %collective-permute-done.9 = bf16[4,3,6,384]{3,2,1,0:T(8,128)(2,1)S(1)} collective-permute-done((bf16[4,3,6,384]{3,2,1,0:T(8,128)(2,1)S(1)}, bf16[4,3,6,384]{3,2,1,0:T(8,128)(2,1)S(1)}, u32[]{:S(2)}, u32[]{:S(2)}) %collective-permute-start.9) | collective-permute-done | bytes 55328 | tf_op jit(solution)/shard_map/ppermute | solution.py:17
  (207 shorter events, 42.9 us)
Async XLA Ops:
  0.0 331.1 %copy-start = (bf16[384,1152]{1,0:T(8,128)(2,1)S(1)}, bf16[384,1152]{1,0:T(8,128)(2,1)}, u32[]{:S(2)}) copy-start(bf16[384,1152]{1,0:T(8,128)(2,1)} %param.35) | copy-start | bytes 2654212
  0.0 13.3 %copy-start.22 = (s32[96]{0:T(128)S(1)}, s32[96]{0:T(128)}, u32[]{:S(2)}) copy-start(s32[96]{0:T(128)} %param.24) | copy-start | bytes 1156
  0.0 13.7 %copy-start.15 = (s32[4,12,12]{2,0,1:T(4,128)S(1)}, s32[4,12,12]{2,0,1:T(4,128)}, u32[]{:S(2)}) copy-start(s32[4,12,12]{2,0,1:T(4,128)} %param.22) | copy-start | bytes 6916
  2.4 11.4 %collective-permute-start = (bf16[4,3,12,192]{3,0,2,1:T(4,128)(2,1)S(1)}, bf16[4,3,12,192]{3,0,2,1:T(4,128)(2,1)S(1)}, u32[]{:S(2)}, u32[]{:S(2)}) collective-permute-start(bf16[4,3,12,192]{3,0,2,1:T(4,128)(2,1)S(1)} %pad_maximum_fusion.7), channel_id=1, source_target_pairs={{64,0},{128,64},{192,128},{256,192},{320,256},{384,320},{448,384},... | collective-permute-start | bytes 165896 | tf_op jit(solution)/shard_map/ppermute | solution.py:17
  9.6 312.3 %collective-permute-start.7 = (bf16[4,6,6]{2,0,1:T(4,128)(2,1)S(1)}, bf16[4,6,6]{2,0,1:T(4,128)(2,1)S(1)}, u32[]{:S(2)}, u32[]{:S(2)}) collective-permute-start(bf16[4,6,6]{2,0,1:T(4,128)(2,1)S(1)} %convert_element_type.165), channel_id=1, source_target_pairs={{0,1},{1,0},{2,3},{3,2},{4,5},{5,4},{6,7},{7,6},{8,9},{9,8},{10,11... | collective-permute-start | bytes 872 | tf_op jit(solution)/shard_map/ppermute | solution.py:27
  13.8 14.8 %copy-start.18 = (f32[192]{0:T(256)S(1)}, f32[192]{0:T(256)}, u32[]{:S(2)}) copy-start(f32[192]{0:T(256)} %param.25) | copy-start | bytes 2308
  14.0 12.7 %collective-permute-start.1 = (bf16[4,12,6,192]{3,0,2,1:T(4,128)(2,1)S(1)}, bf16[4,12,6,192]{3,0,2,1:T(4,128)(2,1)S(1)}, u32[]{:S(2)}, u32[]{:S(2)}) collective-permute-start(bf16[4,12,6,192]{3,0,2,1:T(4,128)(2,1)S(1)} %get-tuple-element.205), channel_id=1, source_target_pairs={{1,0},{2,1},{3,2},{4,3},{5,4},{6,5},{7,6},{8,7},{9,8},{10,9},{11,1... | collective-permute-start | bytes 331784 | tf_op jit(solution)/shard_map/ppermute | solution.py:17
  24.8 4.6 %copy-start.1 = (bf16[192,576]{1,0:T(8,128)(2,1)S(1)}, bf16[192,576]{1,0:T(8,128)(2,1)}, u32[]{:S(2)}) copy-start(bf16[192,576]{1,0:T(8,128)(2,1)} %param.26) | copy-start | bytes 663556
  24.8 4.6 %copy-start.4 = (s32[20736]{0:T(1024)S(1)}, s32[20736]{0:T(1024)}, u32[]{:S(2)}) copy-start(s32[20736]{0:T(1024)} %constant.228) | copy-start | bytes 248836
  29.4 80.7 %copy-start.2 = (bf16[2,2,1,144,192]{4,1,3,0,2:T(2,128)(2,1)}, bf16[2,2,1,144,192]{4,1,3,0,2:T(2,128)(2,1)S(1)}, u32[]{:S(2)}) copy-start(bf16[2,2,1,144,192]{4,1,3,0,2:T(2,128)(2,1)S(1)} %get-tuple-element.293) | copy-start | bytes 663556 | tf_op jit(solution)/shard_map/while
  114.6 2.0 copy-start.3
  114.6 2.0 copy-start.5
  116.6 80.7 %copy-start.2 = (bf16[2,2,1,144,192]{4,1,3,0,2:T(2,128)(2,1)}, bf16[2,2,1,144,192]{4,1,3,0,2:T(2,128)(2,1)S(1)}, u32[]{:S(2)}) copy-start(bf16[2,2,1,144,192]{4,1,3,0,2:T(2,128)(2,1)S(1)} %get-tuple-element.293) | copy-start | bytes 663556 | tf_op jit(solution)/shard_map/while
  201.7 2.0 copy-start.3
  201.7 2.0 copy-start.5
  203.7 21.3 %copy-start.7 = (bf16[4,12,12,192]{3,0,2,1:T(4,128)(2,1)S(1)}, bf16[4,12,12,192]{3,0,2,1:T(4,128)(2,1)}, u32[]{:S(2)}) copy-start(bf16[4,12,12,192]{3,0,2,1:T(4,128)(2,1)} %param.21) | copy-start | bytes 663556
  205.3 20.8 %copy-start.19 = (f32[192]{0:T(256)S(1)}, f32[192]{0:T(256)}, u32[]{:S(2)}) copy-start(f32[192]{0:T(256)} %param.29) | copy-start | bytes 2308
  205.3 10.8 %collective-permute-start.2 = (bf16[4,12,6,192]{3,0,2,1:T(4,128)(2,1)S(1)}, bf16[4,12,6,192]{3,0,2,1:T(4,128)(2,1)S(1)}, u32[]{:S(2)}, u32[]{:S(2)}) collective-permute-start(bf16[4,12,6,192]{3,0,2,1:T(4,128)(2,1)S(1)} %get-tuple-element.202), channel_id=1, source_target_pairs={{63,0},{0,1},{1,2},{2,3},{3,4},{4,5},{5,6},{6,7},{7,8},{8,9},{9,10... | collective-permute-start | bytes 331784 | tf_op jit(solution)/shard_map/ppermute | solution.py:17
  216.2 8.4 %collective-permute-start.3 = (bf16[4,3,12,192]{3,0,2,1:T(4,128)(2,1)S(1)}, bf16[4,3,12,192]{3,0,2,1:T(4,128)(2,1)S(1)}, u32[]{:S(2)}, u32[]{:S(2)}) collective-permute-start(bf16[4,3,12,192]{3,0,2,1:T(4,128)(2,1)S(1)} %pad_maximum_fusion.6), channel_id=1, source_target_pairs={{448,0},{0,64},{64,128},{128,192},{192,256},{256,320},{320,384},{3... | collective-permute-start | bytes 165896 | tf_op jit(solution)/shard_map/ppermute | solution.py:17
  225.6 1.1 copy-start.20
  225.6 1.1 copy-start.21
  231.6 2.1 copy-start.9
  231.6 2.1 copy-start.16
  232.7 4.2 %copy-start.13 = (bf16[1,2,12,3312]{3,1,2,0:T(2,128)(2,1)S(1)}, bf16[1,2,12,3312]{3,1,2,0:T(2,128)(2,1)}, u32[]{:S(2)}) copy-start(bf16[1,2,12,3312]{3,1,2,0:T(2,128)(2,1)} %param.37) | copy-start | bytes 476932
  234.0 5.2 %copy-start.8 = (s32[21504]{0:T(1024)S(1)}, s32[21504]{0:T(1024)}, u32[]{:S(2)}) copy-start(s32[21504]{0:T(1024)} %pad_clamp_fusion.1) | copy-start | bytes 258052
  234.2 87.7 %collective-permute-start.4 = (bf16[4,3,6,384]{3,2,1,0:T(8,128)(2,1)S(1)}, bf16[4,3,6,384]{3,2,1,0:T(8,128)(2,1)S(1)}, u32[]{:S(2)}, u32[]{:S(2)}) collective-permute-start(bf16[4,3,6,384]{3,2,1,0:T(8,128)(2,1)S(1)} %get-tuple-element.209), channel_id=1, source_target_pairs={{64,0},{128,64},{192,128},{256,192},{320,256},{384,320},{448,384},... | collective-permute-start | bytes 165896 | tf_op jit(solution)/shard_map/ppermute | solution.py:17
  316.1 7.8 %copy-start.14 = (s32[4,6,6]{2,0,1:T(4,128)S(1)}, s32[4,6,6]{2,0,1:T(4,128)}, u32[]{:S(2)}) copy-start(s32[4,6,6]{2,0,1:T(4,128)} %param.23) | copy-start | bytes 1732
  316.1 11.3 %copy-start.17 = (f32[384]{0:T(512)S(1)}, f32[384]{0:T(512)}, u32[]{:S(2)}) copy-start(f32[384]{0:T(512)} %param.34) | copy-start | bytes 4612
  322.0 4.6 %collective-permute-start.5 = (bf16[4,6,6,384]{3,2,1,0:T(8,128)(2,1)S(1)}, bf16[4,6,6,384]{3,2,1,0:T(8,128)(2,1)S(1)}, u32[]{:S(2)}, u32[]{:S(2)}) collective-permute-start(bf16[4,6,6,384]{3,2,1,0:T(8,128)(2,1)S(1)} %pad_maximum_fusion.5), channel_id=1, source_target_pairs={{1,0},{2,1},{3,2},{4,3},{5,4},{6,5},{7,6},{8,7},{9,8},{10,9},{11,1... | collective-permute-start | bytes 331784 | tf_op jit(solution)/shard_map/ppermute | solution.py:17
  327.6 3.3 collective-permute-start.6
  338.8 13.0 %collective-permute-start.8 = (bf16[4,6,6,384]{3,2,1,0:T(8,128)(2,1)S(1)}, bf16[4,6,6,384]{3,2,1,0:T(8,128)(2,1)S(1)}, u32[]{:S(2)}, u32[]{:S(2)}) collective-permute-start(bf16[4,6,6,384]{3,2,1,0:T(8,128)(2,1)S(1)} %constant_dynamic-slice_fusion.2), channel_id=1, source_target_pairs={{63,0},{0,1},{1,2},{2,3},{3,4},{4,5},{5,6},{6,7},{7,8},{8,9},{9,10... | collective-permute-start | bytes 331784 | tf_op jit(solution)/shard_map/ppermute | solution.py:17
  351.8 8.4 %collective-permute-start.9 = (bf16[4,3,6,384]{3,2,1,0:T(8,128)(2,1)S(1)}, bf16[4,3,6,384]{3,2,1,0:T(8,128)(2,1)S(1)}, u32[]{:S(2)}, u32[]{:S(2)}) collective-permute-start(bf16[4,3,6,384]{3,2,1,0:T(8,128)(2,1)S(1)} %get-tuple-element.206), channel_id=1, source_target_pairs={{448,0},{0,64},{64,128},{128,192},{192,256},{256,320},{320,384},{3... | collective-permute-start | bytes 165896 | tf_op jit(solution)/shard_map/ppermute | solution.py:17
  (7 other events, 6.5 us)
where the time goes:
time: 363 us; the launch traced here: 361 us
  local copies, waits for them, and re-layouts  267 us (74%)
  waiting for transfers between devices  36.8 us (10%)
  starting transfers between devices  34 us (9%)
  other arithmetic  11.4 us (3%)
  matrix products  11 us (3%)
    gather x6, local copies, waits for them, and re-layouts, one_band(): bias = jnp.take(table_win, index_table, axis=2).astype(jnp.float32)  217 us
    ppermute x8, waiting for transfers between devices, from_behind(): return lax.ppermute(block, axis, route)  35.6 us
    ppermute x8, starting transfers between devices, from_behind(): return lax.ppermute(block, axis, route)  30.2 us
    convert_element_type x6, local copies, waits for them, and re-layouts, one_band(): bias = jnp.take(table_win, index_table, axis=2).astype(jnp.float32)  19.8 us
  transfers between devices with their start and end apart: 10, of which 7 were waited for; matrix products, arithmetic and copies ran while one was open for 76% of the time, Pallas kernels for 0%

commit v1 on v0

v1 whole, which is shorter than its diff:
```python
import functools

import jax
import jax.numpy as jnp
import ml_dtypes
import numpy as np
from jax import lax
from jax.experimental import pallas as pl
from jax.experimental.pallas import tpu as pltpu
from jax.sharding import PartitionSpec as P

D1, H1, MLP = 192, 6, 768
D2, H2 = 384, 12
HEAD = 32
LIVE = 36
HELD = 48
KEYS = 4 * LIVE
COLUMN = 6 * LIVE
PAIRS = 3312
SPAN = 6 * 23
TABLE = 3456
FAR = 2.0**100
MESH = pl.DeviceIdType.MESH
LEVELS = ((1, 2), (3, 0))
FEATURE = 64


def atom_rows():
    return [((z * 3 + a) * 6 + o, z, a, o) for z in range(2) for a in range(3) for o in range(6)]


@functools.lru_cache(None)
def constants():
    split = np.zeros((2, 2, 40, 3, 12, 8), np.float32)
    for level in range(2):
        for og in range(2):
            for r, z, a, o in atom_rows():
                split[level, og, r, a, og * 6 + o, LEVELS[level][z]] = 1

    def spread(heads):
        rows = np.zeros((6, heads, 6, HELD), np.float32)
        for r, z, a, o in atom_rows():
            rows[o, :, z * 3 + a, r] = 1
        return rows.reshape(-1, HELD)

    def head_mask(heads, lanes):
        mask = np.zeros((6, heads, 6, lanes), np.float32)
        for h in range(heads):
            mask[:, h, :, h * HEAD : (h + 1) * HEAD] = 1
        mask[..., heads * HEAD :] = 1
        return mask.reshape(-1, lanes)

    def choose(heads, padded):
        sel = np.zeros((2, 2, heads, 6, 2, 6, padded), np.float32)
        for level in range(2):
            for s in range(2):
                for h in range(heads):
                    for za in range(6):
                        sel[level, s, h, za, s, za, 2 * h + level] = 1
        return sel.reshape(4 * heads * 6, 2 * 6 * padded)

    shift = np.zeros((2, 3, 512, KEYS), np.float32)
    for half in range(2):
        for pair in range(3):
            oq = 6 * half + 2 * pair
            for ah in range(2):
                for oh in range(2):
                    for r, z, a, o in atom_rows():
                        lane = z * 256 + (3 * ah + a) * 23 + oq - (6 * oh + o) + 11
                        shift[half, pair, lane, (oh * 2 + ah) * LIVE + r] = 1

    repeat = np.zeros((128, 128), np.float32)
    level_lanes = np.zeros((12, 8, 128), np.float32)
    gather = np.zeros((16, 12, 8), np.float32)
    for z in range(4):
        for n in range(32):
            repeat[n, z * 32 + n] = 1
        level_lanes[:, z, z * 32 : z * 32 + 32] = 1
        for a in range(12):
            gather[a, a, z] = 1
    rows_one = np.zeros((COLUMN, 32), np.float32)
    rows_two = np.zeros((COLUMN, 32), np.float32)
    table = np.zeros((11, COLUMN, 128), np.float32)
    table[8:10, :, FEATURE : FEATURE + 4] = 1
    table[8:10, :, FEATURE + 5 : FEATURE + 25] = 1
    for ag in range(6):
        for r, z, a, o in atom_rows():
            k = ag * LIVE + r
            window, ah = ag // 2, ag % 2
            rows_one[k, (0 if window == 0 else 16) + (6, 0, 6)[window] + 3 * ah + a] = 1
            if ag < 4:
                rows_two[k, 16 * window + 3 * ah + a] = 1
            table[10, k, :] = 3 * ag + a
            for level in range(2):
                table[4 + level, k, (2 * level + z) * 32 + 16 + o] = 1
                for oh in range(2):
                    table[2 * level + oh, k, (2 * level + z) * 32 + 6 * oh + o] = 1
            for oh in range(2):
                for at in (5 + z, 7 + 3 * ah + a, 13 + 6 * oh + o):
                    table[6 + oh, k, FEATURE + at] = 1
                    table[8 + oh, k, FEATURE + at] = 0

    merge = np.zeros((4, 2, LIVE, 2, 4, LIVE), np.float32)
    for da in range(2):
        for do in range(2):
            for half in range(2):
                for r, z, a, o in atom_rows():
                    row, col = 2 * (3 * half + a) + da, 2 * o + do
                    at = (z * 3 + row % 3) * 6 + col % 6
                    merge[da * 2 + do, half, r, col // 6, row // 3, at] = 1
    final = np.zeros((6, 6, 8, 2, 2, LIVE), np.float32)
    for level in range(2):
        for half in range(2):
            for r, z, a, o in atom_rows():
                final[3 * half + a, o, LEVELS[level][z], level, half, r] = 1
    b = lambda x: x.astype(ml_dtypes.bfloat16)
    flip = lambda x: np.concatenate([x.T[:LIVE], np.zeros((4, x.shape[0]), np.float32)])
    return dict(
        split=b(split.reshape(160, 288)),
        repeat=b(repeat),
        level_lanes=level_lanes.reshape(96, 128),
        gather=b(gather.reshape(16, 96)),
        choose_one=b(choose(H1, 16)),
        choose_two=b(choose(H2, 24)),
        shift=b(shift),
        rows_one=b(rows_one),
        rows_two=b(rows_two),
        table=table,
        spread_one=b(spread(H1)),
        heads_one=b(head_mask(H1, 256)),
        back_one=b(flip(spread(H1))),
        merge=b(merge.reshape(288, 288)),
        spread_two=b(spread(H2)),
        heads_two=b(head_mask(H2, 512)),
        back_two=b(flip(spread(H2))),
        final=b(final.reshape(288, 144)),
    )


CONST_NAMES = tuple(constants())
ARG_NAMES = (
    "fields",
    "region_one",
    "region_two",
    "valid",
    "gain_one",
    "project_one",
    "output_one",
    "table_one",
    "gain_two",
    "up",
    "down",
    "gain_three",
    "merge_weight",
    "gain_four",
    "project_two",
    "output_two",
    "table_two",
)
FETCHED = (
    "fields",
    "split",
    "region_one",
    "region_two",
    "repeat",
    "level_lanes",
    "gather",
    "table_one",
    "choose_one",
    "shift",
    "project_one",
    "rows_one",
    "table",
    "table_two",
    "choose_two",
    "spread_one",
    "heads_one",
    "back_one",
    "output_one",
    "up",
    "down",
    "merge",
    "merge_weight",
    "project_two",
    "rows_two",
    "spread_two",
    "heads_two",
    "back_two",
    "output_two",
    "final",
)


def dot(a, b):
    return jnp.dot(a, b, preferred_element_type=jnp.float32)


def dot_t(a, b):
    return lax.dot_general(a, b, (((1,), (1,)), ((), ())), preferred_element_type=jnp.float32)


def bf(x):
    return x.astype(jnp.bfloat16)


def normalize(x, gain):
    x = x.astype(jnp.float32)
    x = x - jnp.mean(x, -1, keepdims=True)
    var = jnp.mean(x * x, -1, keepdims=True)
    return bf(x * lax.rsqrt(var + 1e-5) * gain)


def attend(q, spread, head_mask, key, bias, value, back):
    q = bf(dot(spread, bf(q))) * head_mask
    scores = dot_t(q, key) + bias
    weights = jnp.exp(scores - jnp.max(scores, -1, keepdims=True))
    probs = bf(weights * (1.0 / jnp.sum(weights, -1, keepdims=True)))
    mixed = bf(dot(probs, value)) * head_mask[:, 0 : value.shape[1]]
    return dot(back, mixed)[0:LIVE]


def kernel(lat_size, lon_size, names, scratch_names, *refs):
    g = dict(zip((*names, "out", *scratch_names), refs, strict=True))
    send, recv, load = g["send"], g["recv"], g["load"]
    lat, lon = lax.axis_index("lat"), lax.axis_index("lon")
    odd = lax.rem(lon, 2)
    half_own = 1 - odd

    def at(dlat, dlon):
        return (lax.rem(lat + dlat + lat_size, lat_size), lax.rem(lon + dlon + lon_size, lon_size))

    around = [(a, o) for a in (-1, 0, 1) for o in (-1, 0, 1) if (a, o) != (0, 0)]
    barrier = pltpu.get_barrier_semaphore()
    for a, o in around + [(0, -2), (-1, -2)]:
        pl.semaphore_signal(barrier, inc=1, device_id=at(a, o), device_id_type=MESH)

    loads = {}
    for n, name in enumerate(FETCHED):
        loads[name] = pltpu.make_async_copy(g[name], g["vmem_" + name], load.at[n])
        loads[name].start()
    ready = set()

    def v(name):
        if name not in loads:
            return g[name]
        if name not in ready:
            loads[name].wait()
            ready.add(name)
        return g["vmem_" + name]

    copies = []

    def start(src, dst, target):
        n = len(copies)
        copy = pltpu.make_async_remote_copy(
            src_ref=src, dst_ref=dst, send_sem=send.at[n], recv_sem=recv.at[n], device_id=target, device_id_type=MESH
        )
        copies.append(copy)
        copy.start()
        return copy

    ext, rows_in = g["ext"], g["rows_in"]
    rows_in[...] = jnp.zeros_like(rows_in)
    for a in range(12):
        rows_in[a, :, 0:4, :] = v("fields")[a].astype(jnp.float32)
    for ag in range(4):
        moved = dot(v("split")[...], bf(rows_in[3 * ag : 3 * ag + 3].reshape(288, D1)))
        for level in range(2):
            for og in range(2):
                lo = (level * 2 + og) * 40
                ext[level, 1 + og, (1 + ag) * LIVE : (2 + ag) * LIVE, :] = moved[lo : lo + LIVE]

    def pack_level(level):
        for og in range(2):
            x = ext[level, 1 + og, LIVE : 5 * LIVE, :]
            tail = jnp.concatenate([x[0:72, 128:192], x[72:144, 128:192]], 1)
            tail = jnp.concatenate([tail, jnp.zeros((8, 128), jnp.float32)], 0)
            g["send_lon"][level, og] = bf(jnp.concatenate([x[:, 0:128], tail], 0))
        for end in range(2):
            lo = (1 + 3 * end) * LIVE
            x, y = ext[level, 1, lo : lo + 40, :], ext[level, 2, lo : lo + 40, :]
            tail = jnp.concatenate([x[:, 128:192], y[:, 128:192]], 1)
            g["send_lat"][level, end] = bf(
                jnp.concatenate([x[:, 0:128], y[:, 0:128], tail, jnp.zeros((8, 128), jnp.float32)], 0)
            )
            zero = jnp.zeros((40, 64), jnp.float32)
            for og, part in enumerate((x, y)):
                g["send_corner"][level, 2 * end + og] = bf(
                    jnp.concatenate([part[:, 0:128], jnp.concatenate([part[:, 128:192], zero], 1)], 0)
                )

    def send_level(level):
        lon_s, lat_s, cor_s = g["send_lon"], g["send_lat"], g["send_corner"]
        lon_r, lat_r, cor_r = g["recv_lon"], g["recv_lat"], g["recv_corner"]
        return [
            start(lon_s.at[level, 0], lon_r.at[level, 1], at(0, -1)),
            start(lon_s.at[level, 1], lon_r.at[level, 0], at(0, 1)),
            start(lat_s.at[level, 0], lat_r.at[level, 1], at(-1, 0)),
            start(lat_s.at[level, 1], lat_r.at[level, 0], at(1, 0)),
            start(cor_s.at[level, 0], cor_r.at[level, 3], at(-1, -1)),
            start(cor_s.at[level, 1], cor_r.at[level, 2], at(-1, 1)),
            start(cor_s.at[level, 2], cor_r.at[level, 1], at(1, -1)),
            start(cor_s.at[level, 3], cor_r.at[level, 0], at(1, 1)),
        ]

    def unpack_level(level):
        for side in range(2):
            x = g["recv_lon"][level, side].astype(jnp.float32)
            c = 3 * side
            ext[level, c, LIVE : 5 * LIVE, 0:128] = x[0:144]
            ext[level, c, LIVE : 3 * LIVE, 128:192] = x[144:216, 0:64]
            ext[level, c, 3 * LIVE : 5 * LIVE, 128:192] = x[144:216, 64:128]
            for end in range(2):
                y = g["recv_corner"][level, 2 * end + side].astype(jnp.float32)
                lo = 5 * LIVE * end
                ext[level, c, lo : lo + LIVE, 0:128] = y[0:LIVE]
                ext[level, c, lo : lo + LIVE, 128:192] = y[40 : 40 + LIVE, 0:64]
        for end in range(2):
            x = g["recv_lat"][level, end].astype(jnp.float32)
            lo = 5 * LIVE * end
            for og in range(2):
                ext[level, 1 + og, lo : lo + LIVE, 0:128] = x[og * 40 : og * 40 + LIVE]
                ext[level, 1 + og, lo : lo + LIVE, 128:192] = x[80 : 80 + LIVE, og * 64 : og * 64 + 64]

    pack_level(0)
    pl.semaphore_wait(barrier, 10)
    first = [send_level(0)]

    ids, region = g["ids"], g["region"]
    region[...] = jnp.zeros_like(region)
    region[:, 0:4, 0:12] = v("region_one")[...].astype(jnp.float32)
    region[0:6, 0:4, 16:22] = v("region_two")[...].astype(jnp.float32)
    packed = dot(bf(region[...].reshape(96, 128)), v("repeat")[...]) * v("level_lanes")[...]
    ids[0] = bf(dot(v("gather")[...], bf(packed)))
    id_copies = [
        start(ids.at[0], ids.at[1], at(1, 0)),
        start(ids.at[0], ids.at[2], at(0, 1)),
        start(ids.at[0], ids.at[3], at(1, 1)),
        start(ids.at[0], ids.at[4], at(0, 2)),
        start(ids.at[0], ids.at[5], at(1, 2)),
    ]
    table_copy_one = start(v("table_one").at[1], g["table_in_one"], at(1, 0))
    pack_level(1)
    first.append(send_level(1))
    table_copy_two = start(v("table_two").at[0], g["table_in_two"], at(1, 0))

    lane_one = lax.broadcasted_iota(jnp.int32, (D1, 256), 1)
    weight = v("project_one")[...].astype(jnp.float32)
    weight_kv, weight_q = g["weight_kv"], g["weight_q"]
    shifted = pltpu.roll(weight[:, 128:512], 384 - 64, 1)[:, 0:256]
    weight_kv[:, 0:256] = bf(jnp.where(lane_one < D1, shifted, 0.0))
    weight_kv[:, 256:448] = bf(weight[:, 384:576])
    weight_q[...] = bf(jnp.where(lane_one < D1, weight[:, 0:256], 0.0))

    def window_rows(flat, window, first_row):
        parts = []
        for shift in range(2):
            for zq in range(2):
                for aq in range(first_row, first_row + 3):
                    pieces = []
                    for zk in range(2):
                        offset = ((zq * 2 + zk) * 6 + aq) * SPAN + shift
                        base = offset // 128 * 128
                        piece = flat[window, :, base : base + 384]
                        if offset != base:
                            piece = pltpu.roll(piece, 384 - (offset - base), 1)
                        pieces.append(piece[:, 0:256])
                    parts.append(jnp.concatenate(pieces, 1))
        return bf(jnp.concatenate(parts, 0))

    flat_one, flat_two = g["flat_one"], g["flat_two"]
    left_one, left_two, bias_one, bias_two = g["left_one"], g["left_two"], g["bias_one"], g["bias_two"]
    flat_one[...] = jnp.zeros_like(flat_one)
    flat_two[...] = jnp.zeros_like(flat_two)

    def fill_one(ag):
        window, first_row = ((0, 3), (1, 0), (1, 3), (2, 0))[ag]
        part = dot(v("choose_one")[...], window_rows(flat_one, window, first_row))
        for level in range(2):
            left_one[level * 288 + ag * 72 : level * 288 + ag * 72 + 72] = part[level * 72 : level * 72 + 72]

    def fill_two(ag):
        part = dot(v("choose_two")[...], window_rows(flat_two, ag, 3 - 3 * ag))
        for level in range(2):
            lo = (level * 2 + ag) * 144
            left_two[lo : lo + 144] = part[level * 144 : level * 144 + 144]

    for h in range(H1):
        for window in (1, 2):
            flat_one[window, 2 * h : 2 * h + 2, 0:PAIRS] = v("table_one")[window - 1, h].astype(jnp.float32)
    for ag in (1, 2, 3):
        fill_one(ag)
    for h in range(H2):
        flat_two[1, 2 * h : 2 * h + 2, 0:PAIRS] = v("table_two")[0, h].astype(jnp.float32)
    fill_two(1)
    table_copy_one.wait_recv()
    for h in range(H1):
        flat_one[0, 2 * h : 2 * h + 2, 0:PAIRS] = g["table_in_one"][h].astype(jnp.float32)
    fill_one(0)
    left = bf(left_one[...])
    for og in range(2):
        for pair in range(3):
            part = dot(left, v("shift")[1 - og, pair])
            for block in range(8):
                bias_one[block, og, pair * 72 : pair * 72 + 72] = part[block * 72 : block * 72 + 72]

    for copy in id_copies:
        copy.wait_recv()
    table = v("table")
    valid = g["valid"][...]
    rows_global = valid.shape[1]
    lane_valid = lax.broadcasted_iota(jnp.int32, (COLUMN, rows_global), 1)
    lane_number = lax.broadcasted_iota(jnp.int32, (COLUMN, 128), 1).astype(jnp.float32)
    row_here = table[10, :, 0:rows_global].astype(jnp.int32)

    def wrap(row, extent):
        return jnp.where(row >= extent, row - extent, row)

    row = wrap(lax.rem(12 * lat + rows_global - 3, rows_global) + row_here, rows_global)
    alive = jnp.sum(jnp.where((lane_valid == row) & (valid == 1), 1.0, 0.0), -1, keepdims=True)
    row = wrap(lax.rem(6 * lat + rows_global // 2 - 3, rows_global // 2) + row_here, rows_global // 2)
    alive_two = jnp.max(jnp.where((lane_valid >> 1 == row) & (valid == 1), 1.0, 0.0), -1, keepdims=True)
    for side in range(2):
        mine = jnp.concatenate([ids[3 - 2 * side], ids[2 - 2 * side]], 0)
        picked = dot(v("rows_one")[...], mine)
        for level in range(2):
            for oh in range(2):
                c = 2 * side + oh
                number = jnp.sum(picked * table[2 * level + oh], -1, keepdims=True)
                same = jnp.where(number + FEATURE == lane_number, 1.0, 0.0)
                g["key_mask"][level, c] = same + (1.0 - alive) * table[6 + oh]
                if c in (1, 2):
                    g["query_mask"][level, c - 1] = (table[8 + oh] - same) * (-FAR)
    for oh in range(2):
        slot = 2 * half_own + 2 - 2 * oh
        mine = jnp.concatenate([ids[slot + 1], ids[slot]], 0)
        picked = dot(v("rows_two")[...], mine)
        for level in range(2):
            number = jnp.sum(picked * table[4 + level], -1, keepdims=True)
            same = jnp.where(number + FEATURE == lane_number, 1.0, 0.0)
            g["key_mask_two"][level, oh] = same + (1.0 - alive_two) * table[6 + oh]
            g["query_mask_two"][level, oh] = (table[8 + oh] - same) * (-FAR)

    kv, queries, heads = g["kv"], g["queries"], g["heads"]

    def section_one(level):
        for c in range(4):
            normed = normalize(ext[level, c], g["gain_one"][...])
            part = dot(normed, weight_kv[...])
            kv[c, :, 0:128] = part[:, 0:128]
            kv[c, :, 128:256] = part[:, 128:256] + g["key_mask"][level, c]
            kv[c, :, 256:448] = part[:, 256:448]
            if c in (1, 2):
                q = dot(normed, weight_q[...]) * HEAD ** (-0.5)
                queries[c - 1, :, 0:128] = q[:, 0:128]
                queries[c - 1, :, 128:256] = q[:, 128:256] + g["query_mask"][level, c - 1]
        for side in range(2):
            for window in range(3):
                lo = window * 72
                both = [kv[2 * side + oh, lo : lo + 72, :] for oh in range(2)]
                both = bf(jnp.concatenate(both, 0))
                key, value = both[:, 0:256], both[:, 256:448]
                for ah in ((1,), (0, 1), (0,))[window]:
                    ag = 2 * window + ah - 1
                    part = attend(
                        queries[side, (ag + 1) * LIVE : (ag + 1) * LIVE + HELD, :],
                        v("spread_one")[...],
                        v("heads_one")[...],
                        key,
                        bias_one[level * 4 + ag, side],
                        value,
                        v("back_one")[...],
                    )
                    base = side * 144 + ag * LIVE
                    heads[base : base + LIVE] = part
        attended = bf(dot(bf(heads[...]), v("output_one")[...]))
        own = jnp.concatenate([ext[level, 1 + og, LIVE : 5 * LIVE, :] for og in range(2)], 0)
        state = bf(own + attended.astype(jnp.float32))
        normed = normalize(state, g["gain_two"][...])
        inner = dot(normed, v("up")[...])
        inner = bf(0.5 * inner * (1.0 + lax.erf(inner * 0.5**0.5)))
        block = bf(state.astype(jnp.float32) + dot_t(inner, v("down")[...]))
        parts = [dot(v("merge")[n * 72 : n * 72 + 72], block) for n in range(4)]
        center = sum(jnp.sum(p, -1, keepdims=True) for p in parts) / (4 * D1)
        parts = [p - center for p in parts]
        scale = lax.rsqrt(sum(jnp.sum(p * p, -1, keepdims=True) for p in parts) / (4 * D1) + 1e-5)
        gain = g["gain_three"][...].reshape(1, 4 * D1)
        coarse = sum(
            dot(bf(parts[n] * scale * gain[:, n * D1 : n * D1 + D1]), v("merge_weight")[n * D1 : n * D1 + D1])
            for n in range(4)
        )
        coarse = bf(coarse).astype(jnp.float32)
        g["ext_two"][level, half_own, LIVE : 3 * LIVE, :] = coarse
        g["coarse"][level] = coarse
        zero = jnp.zeros((8, D2), jnp.float32)
        g["send_all"][level] = bf(jnp.concatenate([coarse, zero], 0))
        g["send_end"][level, 0] = bf(jnp.concatenate([coarse[0:40], zero], 0))
        g["send_end"][level, 1] = bf(jnp.concatenate([coarse[32:72], zero], 0))
        to = 2 * odd - 1
        ends, into = g["send_end"], g["recv_end"]
        return [
            start(g["send_all"].at[level], g["recv_all"].at[level], at(0, to)),
            start(ends.at[level, 0], into.at[level, 0, 1], at(-1, 0)),
            start(ends.at[level, 1], into.at[level, 0, 0], at(1, 0)),
            start(ends.at[level, 0], into.at[level, 1, 1], at(-1, to)),
            start(ends.at[level, 1], into.at[level, 1, 0], at(1, to)),
        ]

    def own_queries(level):
        q = dot(normalize(g["coarse"][level], g["gain_four"][...].reshape(1, D2)), v("project_two")[:, 0:D2]) * HEAD ** (-0.5)
        g["queries_two"][level, 0:72, 0:D2] = q
        g["queries_two"][level, 0:72, D2:512] = g["query_mask_two"][level, half_own, LIVE : 3 * LIVE, :]
        g["queries_two"][level, 72:96, :] = jnp.zeros((24, 512), jnp.float32)

    kv_two, heads_two, ext_two = g["kv_two"], g["heads_two_out"], g["ext_two"]

    def section_two(level):
        ext_two[level, odd, LIVE : 3 * LIVE, :] = g["recv_all"][level].astype(jnp.float32)[0:72]
        for who, oh in ((0, half_own), (1, odd)):
            ext_two[level, oh, 0:LIVE, :] = g["recv_end"][level, who, 0].astype(jnp.float32)[4:40]
            ext_two[level, oh, 3 * LIVE : 4 * LIVE, :] = g["recv_end"][level, who, 1].astype(jnp.float32)[0:LIVE]
        for oh in range(2):
            normed = normalize(ext_two[level, oh], g["gain_four"][...].reshape(1, D2))
            part = dot(normed, v("project_two")[:, D2:])
            kv_two[oh, :, 0:D2] = part[:, 0:D2]
            kv_two[oh, :, D2:512] = g["key_mask_two"][level, oh, 0:144]
            kv_two[oh, :, 512:896] = part[:, D2:]
        for ag in range(2):
            both = bf(jnp.concatenate([kv_two[oh, ag * 72 : ag * 72 + 72, :] for oh in range(2)], 0))
            part = attend(
                g["queries_two"][level, ag * LIVE : ag * LIVE + HELD, :],
                v("spread_two")[...],
                v("heads_two")[...],
                both[:, 0:512],
                bias_two[level * 2 + ag],
                both[:, 512:896],
                v("back_two")[...],
            )
            heads_two[level, ag * LIVE : ag * LIVE + LIVE] = part
        attended = bf(dot(bf(heads_two[level]), v("output_two")[...]))
        return g["coarse"][level] + attended.astype(jnp.float32)

    def wait_all(group):
        for copy in group:
            copy.wait_recv()

    wait_all(first[0])
    unpack_level(0)
    second = [section_one(0)]
    own_queries(0)
    wait_all(first[1])
    unpack_level(1)
    second.append(section_one(1))
    own_queries(1)

    table_copy_two.wait_recv()
    for h in range(H2):
        flat_two[0, 2 * h : 2 * h + 2, 0:PAIRS] = g["table_in_two"][h].astype(jnp.float32)
    fill_two(0)
    left = bf(left_two[...])
    for pair in range(3):
        part = dot(left, v("shift")[half_own, pair])
        for block in range(4):
            bias_two[block, pair * 144 : pair * 144 + 144] = part[block * 144 : block * 144 + 144]

    wait_all(second[0])
    refined = [section_two(0)]
    wait_all(second[1])
    refined.append(section_two(1))
    placed = dot(v("final")[...], bf(jnp.concatenate(refined, 0))).reshape(36, 8, D2)
    for i in range(6):
        g["out"][i] = bf(placed[6 * i : 6 * i + 6, 0:4])
    for copy in copies:
        copy.wait_send()


def shards(lat_size, lon_size, *args):
    operands = dict(zip(ARG_NAMES, args, strict=True))
    for name in ("valid", "gain_one", "gain_two"):
        operands[name] = operands[name][None]
    operands["fields"] = operands["fields"].transpose(1, 2, 0, 3)
    for name in ("region_one", "region_two"):
        operands[name] = operands[name].transpose(1, 0, 2)
    for name in ("table_one", "table_two"):
        operands[name] = operands[name].transpose(0, 2, 1, 3)
    operands["down"] = operands["down"].T
    for name, value in constants().items():
        operands[name] = jnp.asarray(value)
    names = tuple(operands)
    f32, b16 = jnp.float32, jnp.bfloat16
    vmem = pltpu.VMEM
    scratch = dict(
        ext=vmem((2, 4, COLUMN, D1), f32),
        rows_in=vmem((12, 12, 8, D1), f32),
        send_lon=vmem((2, 2, 224, 128), b16),
        recv_lon=vmem((2, 2, 224, 128), b16),
        send_lat=vmem((2, 2, 128, 128), b16),
        recv_lat=vmem((2, 2, 128, 128), b16),
        send_corner=vmem((2, 4, 80, 128), b16),
        recv_corner=vmem((2, 4, 80, 128), b16),
        send_all=vmem((2, 80, D2), b16),
        recv_all=vmem((2, 80, D2), b16),
        send_end=vmem((2, 2, 48, D2), b16),
        recv_end=vmem((2, 2, 2, 48, D2), b16),
        ids=vmem((6, 16, 128), b16),
        region=vmem((12, 8, 128), f32),
        table_in_one=vmem((H1, 2, PAIRS), b16),
        table_in_two=vmem((H2, 2, PAIRS), b16),
        flat_one=vmem((3, 16, TABLE), f32),
        flat_two=vmem((2, 24, TABLE), f32),
        left_one=vmem((576, 512), f32),
        left_two=vmem((576, 512), f32),
        bias_one=vmem((8, 2, 216, KEYS), f32),
        bias_two=vmem((4, 432, KEYS), f32),
        weight_kv=vmem((D1, 448), b16),
        weight_q=vmem((D1, 256), b16),
        key_mask=vmem((2, 4, COLUMN, 128), f32),
        query_mask=vmem((2, 2, COLUMN, 128), f32),
        key_mask_two=vmem((2, 2, COLUMN, 128), f32),
        query_mask_two=vmem((2, 2, COLUMN, 128), f32),
        kv=vmem((4, COLUMN, 448), f32),
        queries=vmem((2, COLUMN, 256), f32),
        heads=vmem((288, D1), f32),
        ext_two=vmem((2, 2, 144, D2), f32),
        coarse=vmem((2, 72, D2), f32),
        kv_two=vmem((2, 144, 896), f32),
        queries_two=vmem((2, 96, 512), f32),
        heads_two_out=vmem((2, 72, D2), f32),
    )
    for name in FETCHED:
        scratch["vmem_" + name] = vmem(operands[name].shape, operands[name].dtype)
    scratch["send"] = pltpu.SemaphoreType.DMA((33,))
    scratch["recv"] = pltpu.SemaphoreType.DMA((33,))
    scratch["load"] = pltpu.SemaphoreType.DMA((len(FETCHED),))
    spec = lambda name: pl.BlockSpec(memory_space=pl.ANY if name in FETCHED else vmem)
    out = pl.pallas_call(
        functools.partial(kernel, lat_size, lon_size, names, tuple(scratch)),
        out_shape=jax.ShapeDtypeStruct((6, 6, 4, D2), b16),
        in_specs=[spec(name) for name in names],
        out_specs=pl.BlockSpec(memory_space=vmem),
        scratch_shapes=list(scratch.values()),
        compiler_params=pltpu.CompilerParams(
            collective_id=0, has_side_effects=True, vmem_limit_bytes=60 * 1024 * 1024
        ),
        name="block",
    )(*operands.values())
    return out.transpose(2, 0, 1, 3)


def solution(mesh):
    split = P(None, "lat", "lon")
    table = P("lat", None, None, None)
    placed = (P(None, "lat", "lon", None), split, split) + (P(),) * 4 + (table,) + (P(),) * 8 + (table,)
    return jax.shard_map(
        functools.partial(shards, mesh.shape["lat"], mesh.shape["lon"]),
        mesh=mesh,
        in_specs=placed,
        out_specs=P(None, "lat", "lon", None),
        check_vma=False,
    )
```

time: 363 us -> 55.4 us (0.15)
  the two profiles are of different devices: /device:TPU:32 before, /device:TPU:1 now
where the time goes in v1:
time: 55.4 us; the launch traced here: 55.2 us
  Pallas kernels  53.6 us (97%)
  local copies, waits for them, and re-layouts  1.58 us (3%)
    pallas_call x1, Pallas kernels, shards(): pl.pallas_call(functools.partial(kernel, lat_size, lon_size, names, tuple...  53.6 us
    unnamed x1, local copies, waits for them, and re-layouts  1.58 us

profile of v1, /device:TPU:1, one launch (start us, length us, event | category | flops | bytes accessed | tf_op | source)
XLA Modules:
  0.0 55.2 jit_solution(7120259137151781473)
XLA Ops:
  0.0 53.6 %block.1 = bf16[6,6,4,384]{3,2,1,0:T(4,128)(2,1)} custom-call(bf16[12,12,4,192]{3,2,1,0:T(4,128)(2,1)} %bitcast.11, s32[12,4,12]{2,1,0:T(4,128)} %bitcast.15, s32[6,4,6]{2,1,0:T(4,128)} %bitcast.16, s32[1,96]{1,0:T(1,128)} %bitcast.19, f32[1,192]{1,0:T(1,128)} %bitcast.17, bf16[192,576]{1,0:T(8,128)(2,1)} %refs_5_.1, bf16[192,192]{1,0:T(8,128)(2,1)} %refs_6_.1, ...), custom_call_target="tpu_custom_call" | custom-call | tf_op jit(solution)/shard_map/block/pallas_call | solution.py:636
  53.6 1.6 %copy.37 = bf16[4,6,6,384]{3,0,2,1:T(4,128)(2,1)} copy(bf16[4,6,6,384]{3,0,2,1:T(4,128)(2,1)} %bitcast.10) | data formatting | bytes 221184

commit v2 on v1

v2 whole, which is shorter than its diff:
```python
import functools
import types

import jax
import jax.numpy as jnp
import ml_dtypes
import numpy as np
from jax import lax
from jax.experimental import pallas as pl
from jax.experimental.pallas import tpu as pltpu
from jax.sharding import PartitionSpec as P

D1, H1, MLP = 192, 6, 768
D2, H2 = 384, 12
HEAD = 32
LIVE = 36
HELD = 48
KEYS = 4 * LIVE
COLUMN = 6 * LIVE
PAIRS = 3312
SPAN = 6 * 23
TABLE = 3456
FAR = 2.0**100
MESH = pl.DeviceIdType.MESH
LEVELS = ((1, 2), (3, 0))
TOGETHER = 8
FEATURE = 64


def atom_rows():
    return [((z * 3 + a) * 6 + o, z, a, o) for z in range(2) for a in range(3) for o in range(6)]


@functools.lru_cache(None)
def constants():
    split = np.zeros((2, 2, 40, 3, 12, 8), np.float32)
    for level in range(2):
        for og in range(2):
            for r, z, a, o in atom_rows():
                split[level, og, r, a, og * 6 + o, LEVELS[level][z]] = 1

    def spread(heads):
        rows = np.zeros((6, heads, 6, HELD), np.float32)
        for r, z, a, o in atom_rows():
            rows[o, :, z * 3 + a, r] = 1
        return rows.reshape(-1, HELD)

    def head_mask(heads, lanes):
        mask = np.zeros((6, heads, 6, lanes), np.float32)
        for h in range(heads):
            mask[:, h, :, h * HEAD : (h + 1) * HEAD] = 1
        mask[..., heads * HEAD :] = 1
        return mask.reshape(-1, lanes)

    def choose(heads, padded):
        sel = np.zeros((2, heads, 6, 6, padded), np.float32)
        for level in range(2):
            for h in range(heads):
                for za in range(6):
                    sel[level, h, za, za, 2 * h + level] = 1
        return sel.reshape(2 * heads * 6, 6 * padded)

    shift = np.zeros((2, KEYS, 512), np.float32)
    for half in range(2):
        for ah in range(2):
            for oh in range(2):
                for r, z, a, o in atom_rows():
                    lane = z * 256 + (3 * ah + a) * 23 + 6 * half - (6 * oh + o) + 11
                    shift[half, (oh * 2 + ah) * LIVE + r, lane] = 1

    repeat = np.zeros((128, 128), np.float32)
    level_lanes = np.zeros((12, 8, 128), np.float32)
    gather = np.zeros((16, 12, 8), np.float32)
    for z in range(4):
        for n in range(32):
            repeat[n, z * 32 + n] = 1
        level_lanes[:, z, z * 32 : z * 32 + 32] = 1
        for a in range(12):
            gather[a, a, z] = 1
    rows_one = np.zeros((COLUMN, 32), np.float32)
    rows_two = np.zeros((COLUMN, 32), np.float32)
    table = np.zeros((11, COLUMN, 128), np.float32)
    table[8:10, :, FEATURE : FEATURE + 4] = 1
    table[8:10, :, FEATURE + 5 : FEATURE + 25] = 1
    for ag in range(6):
        for r, z, a, o in atom_rows():
            k = ag * LIVE + r
            window, ah = ag // 2, ag % 2
            rows_one[k, (0 if window == 0 else 16) + (6, 0, 6)[window] + 3 * ah + a] = 1
            if ag < 4:
                rows_two[k, 16 * window + 3 * ah + a] = 1
            table[10, k, :] = 3 * ag + a
            for level in range(2):
                table[4 + level, k, (2 * level + z) * 32 + 16 + o] = 1
                for oh in range(2):
                    table[2 * level + oh, k, (2 * level + z) * 32 + 6 * oh + o] = 1
            for oh in range(2):
                for at in (5 + z, 7 + 3 * ah + a, 13 + 6 * oh + o):
                    table[6 + oh, k, FEATURE + at] = 1
                    table[8 + oh, k, FEATURE + at] = 0

    merge = np.zeros((4, 2, LIVE, 2, 4, LIVE), np.float32)
    for da in range(2):
        for do in range(2):
            for half in range(2):
                for r, z, a, o in atom_rows():
                    row, col = 2 * (3 * half + a) + da, 2 * o + do
                    at = (z * 3 + row % 3) * 6 + col % 6
                    merge[da * 2 + do, half, r, col // 6, row // 3, at] = 1
    final = np.zeros((6, 6, 8, 2, 2, LIVE), np.float32)
    for level in range(2):
        for half in range(2):
            for r, z, a, o in atom_rows():
                final[3 * half + a, o, LEVELS[level][z], level, half, r] = 1
    b = lambda x: x.astype(ml_dtypes.bfloat16)
    flip = lambda x: np.concatenate([x.T[:LIVE], np.zeros((4, x.shape[0]), np.float32)])
    return dict(
        split=b(split.reshape(160, 288)),
        repeat=b(repeat),
        level_lanes=level_lanes.reshape(96, 128),
        gather=b(gather.reshape(16, 96)),
        choose_one=b(choose(H1, 16)),
        choose_two=b(choose(H2, 24)),
        shift=b(shift),
        rows_one=b(rows_one),
        rows_two=b(rows_two),
        table=table,
        spread_one=b(spread(H1)),
        heads_one=b(head_mask(H1, 256)),
        turned_one=b(head_mask(H1, D1).T),
        back_one=b(flip(spread(H1))),
        merge=b(merge.reshape(288, 288)),
        spread_two=b(spread(H2)),
        heads_two=b(head_mask(H2, 512)),
        turned_two=b(head_mask(H2, D2).T),
        back_two=b(flip(spread(H2))),
        final=b(final.reshape(288, 144)),
    )


def dot(a, b):
    return jnp.dot(a, b, preferred_element_type=jnp.float32)


def dot_t(a, b):
    return lax.dot_general(a, b, (((1,), (1,)), ((), ())), preferred_element_type=jnp.float32)


def bf(x):
    return x.astype(jnp.bfloat16)


def normalize(x, gain):
    x = x.astype(jnp.float32)
    x = x - jnp.mean(x, -1, keepdims=True)
    var = jnp.mean(x * x, -1, keepdims=True)
    return bf(x * lax.rsqrt(var + 1e-5) * gain)


def attend(tasks, spread, head_mask, turned_mask, back):
    qs = [bf(dot(spread, bf(q))) * head_mask for q, _, _, _ in tasks]
    scores = [dot_t(key, q) + bias for q, (_, key, bias, _) in zip(qs, tasks)]
    weights = [jnp.exp(s - jnp.max(s, 0, keepdims=True)) for s in scores]
    probs = [bf(w * (1.0 / jnp.sum(w, 0, keepdims=True))) for w in weights]
    mixed = [bf(dot(value, p)) * turned_mask for p, (_, _, _, value) in zip(probs, tasks)]
    return [dot_t(back, m)[0:LIVE] for m in mixed]


def kernel(lat_size, lon_size, names, fetched, scratch_names, *refs):
    g = types.SimpleNamespace(**dict(zip(names, refs[: len(names)], strict=True)))
    refs = refs[len(names) :]
    g.out = refs[0]
    g.held = dict(zip(fetched, refs[1 : 1 + len(fetched)], strict=True))
    for name, ref in zip(scratch_names, refs[1 + len(fetched) :], strict=True):
        setattr(g, name, ref)
    send, recv, load = g.send, g.recv, g.load
    lat, lon = lax.axis_index("lat"), lax.axis_index("lon")
    odd = lax.rem(lon, 2)
    half_own = 1 - odd

    def at(dlat, dlon):
        return (lax.rem(lat + dlat + lat_size, lat_size), lax.rem(lon + dlon + lon_size, lon_size))

    around = [(a, o) for a in (-1, 0, 1) for o in (-1, 0, 1) if (a, o) != (0, 0)]
    barrier = pltpu.get_barrier_semaphore()
    for a, o in around + [(0, -2), (-1, -2)]:
        pl.semaphore_signal(barrier, inc=1, device_id=at(a, o), device_id_type=MESH)

    class Held:
        def __init__(self):
            self.loads = {}
            for n, name in enumerate(fetched):
                self.loads[name] = pltpu.make_async_copy(getattr(g, name), g.held[name], load.at[n])
                self.loads[name].start()

        def __getattr__(self, name):
            self.loads[name].wait()
            ref = g.held[name]
            setattr(self, name, ref)
            return ref

    v = Held()
    copies = []

    def start(src, dst, target):
        n = len(copies)
        copy = pltpu.make_async_remote_copy(
            src_ref=src, dst_ref=dst, send_sem=send.at[n], recv_sem=recv.at[n], device_id=target, device_id_type=MESH
        )
        copies.append(copy)
        copy.start()
        return copy

    ext, rows_in = g.ext, g.rows_in
    rows_in[...] = jnp.zeros_like(rows_in)
    for a in range(12):
        rows_in[a, :, 0:4, :] = v.fields[a].astype(jnp.float32)
    for ag in range(4):
        moved = dot(v.split[...], bf(rows_in[3 * ag : 3 * ag + 3].reshape(288, D1)))
        for level in range(2):
            for og in range(2):
                lo = (level * 2 + og) * 40
                ext[level, 1 + og, (1 + ag) * LIVE : (2 + ag) * LIVE, :] = moved[lo : lo + LIVE]

    def pack_level(level):
        for og in range(2):
            x = ext[level, 1 + og, LIVE : 5 * LIVE, :]
            tail = jnp.concatenate([x[0:72, 128:192], x[72:144, 128:192]], 1)
            tail = jnp.concatenate([tail, jnp.zeros((8, 128), jnp.float32)], 0)
            g.send_lon[level, og] = bf(jnp.concatenate([x[:, 0:128], tail], 0))
        for end in range(2):
            lo = (1 + 3 * end) * LIVE
            x, y = ext[level, 1, lo : lo + 40, :], ext[level, 2, lo : lo + 40, :]
            tail = jnp.concatenate([x[:, 128:192], y[:, 128:192]], 1)
            g.send_lat[level, end] = bf(
                jnp.concatenate([x[:, 0:128], y[:, 0:128], tail, jnp.zeros((8, 128), jnp.float32)], 0)
            )
            zero = jnp.zeros((40, 64), jnp.float32)
            for og, part in enumerate((x, y)):
                g.send_corner[level, 2 * end + og] = bf(
                    jnp.concatenate([part[:, 0:128], jnp.concatenate([part[:, 128:192], zero], 1)], 0)
                )

    def send_level(level):
        lon_s, lat_s, cor_s = g.send_lon, g.send_lat, g.send_corner
        lon_r, lat_r, cor_r = g.recv_lon, g.recv_lat, g.recv_corner
        return [
            start(lon_s.at[level, 0], lon_r.at[level, 1], at(0, -1)),
            start(lon_s.at[level, 1], lon_r.at[level, 0], at(0, 1)),
            start(lat_s.at[level, 0], lat_r.at[level, 1], at(-1, 0)),
            start(lat_s.at[level, 1], lat_r.at[level, 0], at(1, 0)),
            start(cor_s.at[level, 0], cor_r.at[level, 3], at(-1, -1)),
            start(cor_s.at[level, 1], cor_r.at[level, 2], at(-1, 1)),
            start(cor_s.at[level, 2], cor_r.at[level, 1], at(1, -1)),
            start(cor_s.at[level, 3], cor_r.at[level, 0], at(1, 1)),
        ]

    def unpack_level(level):
        for side in range(2):
            x = g.recv_lon[level, side].astype(jnp.float32)
            c = 3 * side
            ext[level, c, LIVE : 5 * LIVE, 0:128] = x[0:144]
            ext[level, c, LIVE : 3 * LIVE, 128:192] = x[144:216, 0:64]
            ext[level, c, 3 * LIVE : 5 * LIVE, 128:192] = x[144:216, 64:128]
            for end in range(2):
                y = g.recv_corner[level, 2 * end + side].astype(jnp.float32)
                lo = 5 * LIVE * end
                ext[level, c, lo : lo + LIVE, 0:128] = y[0:LIVE]
                ext[level, c, lo : lo + LIVE, 128:192] = y[40 : 40 + LIVE, 0:64]
        for end in range(2):
            x = g.recv_lat[level, end].astype(jnp.float32)
            lo = 5 * LIVE * end
            for og in range(2):
                ext[level, 1 + og, lo : lo + LIVE, 0:128] = x[og * 40 : og * 40 + LIVE]
                ext[level, 1 + og, lo : lo + LIVE, 128:192] = x[80 : 80 + LIVE, og * 64 : og * 64 + 64]

    pack_level(0)
    pl.semaphore_wait(barrier, 10)
    first = [send_level(0)]

    ids, region = g.ids, g.region
    region[...] = jnp.zeros_like(region)
    region[:, 0:4, 0:12] = v.region_one[...].astype(jnp.float32)
    region[0:6, 0:4, 16:22] = v.region_two[...].astype(jnp.float32)
    packed = dot(bf(region[...].reshape(96, 128)), v.repeat[...]) * v.level_lanes[...]
    ids[0] = bf(dot(v.gather[...], bf(packed)))
    id_copies = [
        start(ids.at[0], ids.at[1], at(1, 0)),
        start(ids.at[0], ids.at[2], at(0, 1)),
        start(ids.at[0], ids.at[3], at(1, 1)),
        start(ids.at[0], ids.at[4], at(0, 2)),
        start(ids.at[0], ids.at[5], at(1, 2)),
    ]
    table_copy_one = start(v.table_one.at[1], g.table_in_one, at(1, 0))
    pack_level(1)
    first.append(send_level(1))
    table_copy_two = start(v.table_two.at[0], g.table_in_two, at(1, 0))

    lane_one = lax.broadcasted_iota(jnp.int32, (D1, 256), 1)
    weight = v.project_one[...].astype(jnp.float32)
    weight_k, weight_q = g.weight_k, g.weight_q
    columns = pltpu.roll(weight[:, 128:512], 384 - 64, 1)[:, 0:256]
    weight_k[...] = bf(jnp.where(lane_one < D1, columns, 0.0))
    weight_q[...] = bf(jnp.where(lane_one < D1, weight[:, 0:256], 0.0))
    side = lax.broadcasted_iota(jnp.int32, (D2, D2), 0) == lax.broadcasted_iota(jnp.int32, (D2, D2), 1)
    eye = bf(jnp.where(side, 1.0, 0.0))
    g.turned_v_one[...] = bf(dot_t(eye[0:D1, 0:D1], bf(weight[:, 384:576])))

    def window_rows(flat, window, first_row):
        parts = []
        for zq in range(2):
            for aq in range(first_row, first_row + 3):
                pieces = []
                for zk in range(2):
                    offset = ((zq * 2 + zk) * 6 + aq) * SPAN
                    base = offset // 128 * 128
                    piece = flat[window, :, base : base + 384]
                    if offset != base:
                        piece = pltpu.roll(piece, 384 - (offset - base), 1)
                    pieces.append(piece[:, 0:256])
                parts.append(jnp.concatenate(pieces, 1))
        return bf(jnp.concatenate(parts, 0))

    def shifted(left, block, part):
        rows = part.shape[0]
        for n in range(6):
            moved = pltpu.roll(part, 512 - n, 1) if n else part
            left[block, n * rows : n * rows + rows, :] = moved

    flat_one, flat_two = g.flat_one, g.flat_two
    left_one, left_two, bias_one, bias_two = g.left_one, g.left_two, g.bias_one, g.bias_two
    flat_one[...] = jnp.zeros_like(flat_one)
    flat_two[...] = jnp.zeros_like(flat_two)

    def fill_one(ag):
        window, first_row = ((0, 3), (1, 0), (1, 3), (2, 0))[ag]
        part = dot(v.choose_one[...], window_rows(flat_one, window, first_row))
        for level in range(2):
            block = level * 4 + ag
            shifted(left_one, block, part[level * 36 : level * 36 + 36])
            left = bf(left_one[block])
            for og in range(2):
                bias_one[block, og] = dot_t(v.shift[1 - og], left)

    def fill_two(ag):
        part = dot(v.choose_two[...], window_rows(flat_two, ag, 3 - 3 * ag))
        for level in range(2):
            block = level * 2 + ag
            shifted(left_two, block, part[level * 72 : level * 72 + 72])
            bias_two[block] = dot_t(v.shift[half_own], bf(left_two[block]))

    for h in range(H1):
        for window in (1, 2):
            flat_one[window, 2 * h : 2 * h + 2, 0:PAIRS] = v.table_one[window - 1, h].astype(jnp.float32)
    for ag in (1, 2, 3):
        fill_one(ag)
    for h in range(H2):
        flat_two[1, 2 * h : 2 * h + 2, 0:PAIRS] = v.table_two[0, h].astype(jnp.float32)
    fill_two(1)
    table_copy_one.wait_recv()
    for h in range(H1):
        flat_one[0, 2 * h : 2 * h + 2, 0:PAIRS] = g.table_in_one[h].astype(jnp.float32)
    fill_one(0)

    for copy in id_copies:
        copy.wait_recv()
    table = v.table
    valid = g.valid[...]
    rows_global = valid.shape[1]
    lane_valid = lax.broadcasted_iota(jnp.int32, (COLUMN, rows_global), 1)
    lane_number = lax.broadcasted_iota(jnp.int32, (COLUMN, 128), 1).astype(jnp.float32)
    row_here = table[10, :, 0:rows_global].astype(jnp.int32)

    def wrap(row, extent):
        return jnp.where(row >= extent, row - extent, row)

    row = wrap(lax.rem(12 * lat + rows_global - 3, rows_global) + row_here, rows_global)
    alive = jnp.sum(jnp.where((lane_valid == row) & (valid == 1), 1.0, 0.0), -1, keepdims=True)
    row = wrap(lax.rem(6 * lat + rows_global // 2 - 3, rows_global // 2) + row_here, rows_global // 2)
    alive_two = jnp.max(jnp.where((lane_valid >> 1 == row) & (valid == 1), 1.0, 0.0), -1, keepdims=True)
    for side in range(2):
        mine = jnp.concatenate([ids[3 - 2 * side], ids[2 - 2 * side]], 0)
        picked = dot(v.rows_one[...], mine)
        for level in range(2):
            for oh in range(2):
                c = 2 * side + oh
                number = jnp.sum(picked * table[2 * level + oh], -1, keepdims=True)
                same = jnp.where(number + FEATURE == lane_number, 1.0, 0.0)
                g.key_mask[level, c] = same + (1.0 - alive) * table[6 + oh]
                if c in (1, 2):
                    g.query_mask[level, c - 1] = (table[8 + oh] - same) * (-FAR)
    for oh in range(2):
        slot = 2 * half_own + 2 - 2 * oh
        mine = jnp.concatenate([ids[slot + 1], ids[slot]], 0)
        picked = dot(v.rows_two[...], mine)
        for level in range(2):
            number = jnp.sum(picked * table[4 + level], -1, keepdims=True)
            same = jnp.where(number + FEATURE == lane_number, 1.0, 0.0)
            g.key_mask_two[level, oh] = same + (1.0 - alive_two) * table[6 + oh]
            g.query_mask_two[level, oh] = (table[8 + oh] - same) * (-FAR)

    queries, heads = g.queries, g.heads

    def section_one(level):
        for c in range(4):
            normed = normalize(ext[level, c], g.gain_one[...])
            g.normed_one[c] = normed.astype(jnp.float32)
            if c in (1, 2):
                q = dot(normed, weight_q[...]) * HEAD ** (-0.5)
                queries[c - 1, :, 0:128] = q[:, 0:128]
                queries[c - 1, :, 128:256] = q[:, 128:256] + g.query_mask[level, c - 1]
        places, tasks = [], []
        for side in range(2):
            for window in range(3):
                lo = window * 72
                pair = [g.normed_one[2 * side + oh, lo : lo + 72, :] for oh in range(2)]
                mask = [g.key_mask[level, 2 * side + oh, lo : lo + 72, :] for oh in range(2)]
                tokens = bf(jnp.concatenate(pair, 0))
                key = dot(tokens, weight_k[...])
                key = bf(jnp.concatenate([key[:, 0:128], key[:, 128:256] + jnp.concatenate(mask, 0)], 1))
                value = bf(dot_t(g.turned_v_one[...], tokens))
                for ah in ((1,), (0, 1), (0,))[window]:
                    ag = 2 * window + ah - 1
                    q = queries[side, (ag + 1) * LIVE : (ag + 1) * LIVE + HELD, :]
                    tasks.append((q, key, bias_one[level * 4 + ag, side], value))
                    places.append(side * 144 + ag * LIVE)
        parts = []
        for n in range(0, 8, TOGETHER):
            parts += attend(
                tasks[n : n + TOGETHER], v.spread_one[...], v.heads_one[...], v.turned_one[...], v.back_one[...]
            )
        for place, part in zip(places, parts):
            heads[place : place + LIVE] = part
        attended = bf(dot(bf(heads[...]), v.output_one[...]))
        own = jnp.concatenate([ext[level, 1 + og, LIVE : 5 * LIVE, :] for og in range(2)], 0)
        state = bf(own + attended.astype(jnp.float32))
        normed = normalize(state, g.gain_two[...])
        inner = dot(normed, v.up[...])
        inner = bf(0.5 * inner * (1.0 + lax.erf(inner * 0.5**0.5)))
        block = bf(state.astype(jnp.float32) + dot_t(inner, v.down[...]))
        parts = [dot(v.merge[n * 72 : n * 72 + 72], block) for n in range(4)]
        center = sum(jnp.sum(p, -1, keepdims=True) for p in parts) / (4 * D1)
        parts = [p - center for p in parts]
        scale = lax.rsqrt(sum(jnp.sum(p * p, -1, keepdims=True) for p in parts) / (4 * D1) + 1e-5)
        gain = g.gain_three[...].reshape(1, 4 * D1)
        coarse = sum(
            dot(bf(parts[n] * scale * gain[:, n * D1 : n * D1 + D1]), v.merge_weight[n * D1 : n * D1 + D1])
            for n in range(4)
        )
        coarse = bf(coarse).astype(jnp.float32)
        g.ext_two[level, half_own, LIVE : 3 * LIVE, :] = coarse
        g.coarse[level] = coarse
        zero = jnp.zeros((8, D2), jnp.float32)
        g.send_all[level] = bf(jnp.concatenate([coarse, zero], 0))
        g.send_end[level, 0] = bf(jnp.concatenate([coarse[0:40], zero], 0))
        g.send_end[level, 1] = bf(jnp.concatenate([coarse[32:72], zero], 0))
        to = 2 * odd - 1
        ends, into = g.send_end, g.recv_end
        return [
            start(g.send_all.at[level], g.recv_all.at[level], at(0, to)),
            start(ends.at[level, 0], into.at[level, 0, 1], at(-1, 0)),
            start(ends.at[level, 1], into.at[level, 0, 0], at(1, 0)),
            start(ends.at[level, 0], into.at[level, 1, 1], at(-1, to)),
            start(ends.at[level, 1], into.at[level, 1, 0], at(1, to)),
        ]

    def own_queries(level):
        q = dot(normalize(g.coarse[level], g.gain_four[...].reshape(1, D2)), v.project_two[:, 0:D2]) * HEAD ** (-0.5)
        g.queries_two[level, 0:72, 0:D2] = q
        g.queries_two[level, 0:72, D2:512] = g.query_mask_two[level, half_own, LIVE : 3 * LIVE, :]
        g.queries_two[level, 72:96, :] = jnp.zeros((24, 512), jnp.float32)

    heads_two, ext_two = g.heads_two_out, g.ext_two
    g.turned_v_two[...] = bf(dot_t(eye, v.project_two[:, 2 * D2 :]))

    def section_two(level):
        ext_two[level, odd, LIVE : 3 * LIVE, :] = g.recv_all[level].astype(jnp.float32)[0:72]
        for who, oh in ((0, half_own), (1, odd)):
            ext_two[level, oh, 0:LIVE, :] = g.recv_end[level, who, 0].astype(jnp.float32)[4:40]
            ext_two[level, oh, 3 * LIVE : 4 * LIVE, :] = g.recv_end[level, who, 1].astype(jnp.float32)[0:LIVE]
        for oh in range(2):
            g.normed_two[oh] = normalize(ext_two[level, oh], g.gain_four[...].reshape(1, D2)).astype(jnp.float32)
        tasks = []
        for ag in range(2):
            lo = ag * 72
            tokens = bf(jnp.concatenate([g.normed_two[oh, lo : lo + 72, :] for oh in range(2)], 0))
            mask = jnp.concatenate([g.key_mask_two[level, oh, lo : lo + 72, :] for oh in range(2)], 0)
            tasks.append(
                (
                    g.queries_two[level, ag * LIVE : ag * LIVE + HELD, :],
                    bf(jnp.concatenate([dot(tokens, v.project_two[:, D2 : 2 * D2]), mask], 1)),
                    bias_two[level * 2 + ag],
                    bf(dot_t(g.turned_v_two[...], tokens)),
                )
            )
        parts = attend(tasks, v.spread_two[...], v.heads_two[...], v.turned_two[...], v.back_two[...])
        for ag in range(2):
            heads_two[level, ag * LIVE : ag * LIVE + LIVE] = parts[ag]
        attended = bf(dot(bf(heads_two[level]), v.output_two[...]))
        return g.coarse[level] + attended.astype(jnp.float32)

    def wait_all(group):
        for copy in group:
            copy.wait_recv()

    wait_all(first[0])
    unpack_level(0)
    second = [section_one(0)]
    own_queries(0)
    wait_all(first[1])
    unpack_level(1)
    second.append(section_one(1))
    own_queries(1)

    table_copy_two.wait_recv()
    for h in range(H2):
        flat_two[0, 2 * h : 2 * h + 2, 0:PAIRS] = g.table_in_two[h].astype(jnp.float32)
    fill_two(0)

    wait_all(second[0])
    refined = [section_two(0)]
    wait_all(second[1])
    refined.append(section_two(1))
    placed = dot(v.final[...], bf(jnp.concatenate(refined, 0))).reshape(36, 8, D2)
    for i in range(6):
        g.out[i] = bf(placed[6 * i : 6 * i + 6, 0:4])
    for copy in copies:
        copy.wait_send()


def shards(
    lat_size,
    lon_size,
    fields,
    region_one,
    region_two,
    valid_rows,
    gain_one,
    project_one,
    output_one,
    table_one,
    gain_two,
    up,
    down,
    gain_three,
    merge_weight,
    gain_four,
    project_two,
    output_two,
    table_two,
):
    c = types.SimpleNamespace(**{name: jnp.asarray(value) for name, value in constants().items()})
    direct = dict(
        valid=valid_rows[None],
        gain_one=gain_one[None],
        gain_two=gain_two[None],
        gain_three=gain_three,
        gain_four=gain_four,
    )
    fetched = dict(
        fields=fields.transpose(1, 2, 0, 3),
        split=c.split,
        region_one=region_one.transpose(1, 0, 2),
        region_two=region_two.transpose(1, 0, 2),
        repeat=c.repeat,
        level_lanes=c.level_lanes,
        gather=c.gather,
        table_one=table_one.transpose(0, 2, 1, 3),
        choose_one=c.choose_one,
        shift=c.shift,
        project_one=project_one,
        rows_one=c.rows_one,
        table=c.table,
        table_two=table_two.transpose(0, 2, 1, 3),
        choose_two=c.choose_two,
        rows_two=c.rows_two,
        spread_one=c.spread_one,
        heads_one=c.heads_one,
        turned_one=c.turned_one,
        back_one=c.back_one,
        output_one=output_one,
        up=up,
        down=down.T,
        merge=c.merge,
        merge_weight=merge_weight,
        project_two=project_two,
        spread_two=c.spread_two,
        heads_two=c.heads_two,
        turned_two=c.turned_two,
        back_two=c.back_two,
        output_two=output_two,
        final=c.final,
    )
    operands = direct | fetched
    names = tuple(operands)
    f32, b16 = jnp.float32, jnp.bfloat16
    vmem = pltpu.VMEM
    scratch = dict(
        ext=vmem((2, 4, COLUMN, D1), f32),
        rows_in=vmem((12, 12, 8, D1), f32),
        send_lon=vmem((2, 2, 224, 128), b16),
        recv_lon=vmem((2, 2, 224, 128), b16),
        send_lat=vmem((2, 2, 128, 128), b16),
        recv_lat=vmem((2, 2, 128, 128), b16),
        send_corner=vmem((2, 4, 80, 128), b16),
        recv_corner=vmem((2, 4, 80, 128), b16),
        send_all=vmem((2, 80, D2), b16),
        recv_all=vmem((2, 80, D2), b16),
        send_end=vmem((2, 2, 48, D2), b16),
        recv_end=vmem((2, 2, 2, 48, D2), b16),
        ids=vmem((6, 16, 128), b16),
        region=vmem((12, 8, 128), f32),
        table_in_one=vmem((H1, 2, PAIRS), b16),
        table_in_two=vmem((H2, 2, PAIRS), b16),
        flat_one=vmem((3, 16, TABLE), f32),
        flat_two=vmem((2, 24, TABLE), f32),
        left_one=vmem((8, 216, 512), f32),
        left_two=vmem((4, 432, 512), f32),
        bias_one=vmem((8, 2, KEYS, 216), f32),
        bias_two=vmem((4, KEYS, 432), f32),
        weight_k=vmem((D1, 256), b16),
        turned_v_one=vmem((D1, D1), b16),
        turned_v_two=vmem((D2, D2), b16),
        weight_q=vmem((D1, 256), b16),
        key_mask=vmem((2, 4, COLUMN, 128), f32),
        query_mask=vmem((2, 2, COLUMN, 128), f32),
        key_mask_two=vmem((2, 2, COLUMN, 128), f32),
        query_mask_two=vmem((2, 2, COLUMN, 128), f32),
        normed_one=vmem((4, COLUMN, D1), f32),
        queries=vmem((2, COLUMN, 256), f32),
        heads=vmem((288, D1), f32),
        ext_two=vmem((2, 2, 144, D2), f32),
        coarse=vmem((2, 72, D2), f32),
        normed_two=vmem((2, 144, D2), f32),
        queries_two=vmem((2, 96, 512), f32),
        heads_two_out=vmem((2, 72, D2), f32),
    )
    held = [vmem(x.shape, x.dtype) for x in fetched.values()]
    sems = dict(
        send=pltpu.SemaphoreType.DMA((33,)),
        recv=pltpu.SemaphoreType.DMA((33,)),
        load=pltpu.SemaphoreType.DMA((len(fetched),)),
    )
    spec = lambda name: pl.BlockSpec(memory_space=pl.ANY if name in fetched else vmem)
    scratch |= sems
    out = pl.pallas_call(
        functools.partial(kernel, lat_size, lon_size, names, tuple(fetched), tuple(scratch)),
        out_shape=jax.ShapeDtypeStruct((6, 6, 4, D2), b16),
        in_specs=[spec(name) for name in names],
        out_specs=pl.BlockSpec(memory_space=vmem),
        scratch_shapes=held + list(scratch.values()),
        compiler_params=pltpu.CompilerParams(
            collective_id=0, has_side_effects=True, vmem_limit_bytes=60 * 1024 * 1024
        ),
        name="block",
    )(*operands.values())
    return out.transpose(2, 0, 1, 3)


def solution(mesh):
    split = P(None, "lat", "lon")
    table = P("lat", None, None, None)
    placed = (P(None, "lat", "lon", None), split, split) + (P(),) * 4 + (table,) + (P(),) * 8 + (table,)
    return jax.shard_map(
        functools.partial(shards, mesh.shape["lat"], mesh.shape["lon"]),
        mesh=mesh,
        in_specs=placed,
        out_specs=P(None, "lat", "lon", None),
        check_vma=False,
    )
```

time: 55.4 us -> 46.5 us (0.84)
  Pallas kernels: 53.6 us -> 44.7 us
    pallas_call x1, Pallas kernels: 53.6 us -> 44.7 us  [shards(): pl.pallas_call(functools.partial(kernel, lat_size, lon_size, names, tuple...]
where the time goes in v2:
time: 46.5 us; the launch traced here: 46.3 us
  Pallas kernels  44.7 us (96%)
  local copies, waits for them, and re-layouts  1.58 us (3%)
    pallas_call x1, Pallas kernels, shards(): pl.pallas_call(functools.partial(kernel, lat_size, lon_size, names, tuple...  44.7 us
    unnamed x1, local copies, waits for them, and re-layouts  1.58 us

profile of v2, /device:TPU:1, one launch (start us, length us, event | category | flops | bytes accessed | tf_op | source)
XLA Modules:
  0.0 46.3 jit_solution(753980345313672292)
XLA Ops:
  0.0 44.7 %block.1 = bf16[6,6,4,384]{3,2,1,0:T(4,128)(2,1)} custom-call(s32[1,96]{1,0:T(1,128)} %bitcast.19, f32[1,192]{1,0:T(1,128)} %bitcast.17, f32[1,192]{1,0:T(1,128)} %bitcast.18, f32[768]{0:T(1024)} %refs_3_.1, f32[384]{0:T(512)} %refs_4_.1, bf16[12,12,4,192]{3,2,1,0:T(4,128)(2,1)} %bitcast.11, bf16[160,288]{1,0:T(8,128)(2,1)} %constant.40.clone.refs_6_, ...), custom_call_target="tpu_custom_call" | custom-call | tf_op jit(solution)/shard_map/block/pallas_call | solution.py:646
  44.7 1.6 %copy.39 = bf16[4,6,6,384]{3,0,2,1:T(4,128)(2,1)} copy(bf16[4,6,6,384]{3,0,2,1:T(4,128)(2,1)} %bitcast.10) | data formatting | bytes 221184

commit v3 on v2

--- a/solution.py
+++ b/solution.py
@@ -20,6 +20,7 @@
 PAIRS = 3312
 SPAN = 6 * 23
 TABLE = 3456
+LATER = (384, 1152, 2048, 2816)
 FAR = 2.0**100
 MESH = pl.DeviceIdType.MESH
 LEVELS = ((1, 2), (3, 0))
@@ -222,6 +223,8 @@
                 lo = (level * 2 + og) * 40
                 ext[level, 1 + og, (1 + ag) * LIVE : (2 + ag) * LIVE, :] = moved[lo : lo + LIVE]
 
+    g.stage[...] = jnp.zeros_like(g.stage)
+
     def pack_level(level):
         for og in range(2):
             x = ext[level, 1 + og, LIVE : 5 * LIVE, :]
@@ -230,16 +233,16 @@
             g.send_lon[level, og] = bf(jnp.concatenate([x[:, 0:128], tail], 0))
         for end in range(2):
             lo = (1 + 3 * end) * LIVE
-            x, y = ext[level, 1, lo : lo + 40, :], ext[level, 2, lo : lo + 40, :]
-            tail = jnp.concatenate([x[:, 128:192], y[:, 128:192]], 1)
-            g.send_lat[level, end] = bf(
-                jnp.concatenate([x[:, 0:128], y[:, 0:128], tail, jnp.zeros((8, 128), jnp.float32)], 0)
-            )
-            zero = jnp.zeros((40, 64), jnp.float32)
-            for og, part in enumerate((x, y)):
-                g.send_corner[level, 2 * end + og] = bf(
-                    jnp.concatenate([part[:, 0:128], jnp.concatenate([part[:, 128:192], zero], 1)], 0)
-                )
+            stage = g.stage
+            for og in range(2):
+                stage[og * LIVE : og * LIVE + LIVE, :] = ext[level, 1 + og, lo : lo + LIVE, 0:128]
+            tail = [ext[level, 1 + og, lo : lo + LIVE, 128:192] for og in range(2)]
+            stage[72:108, :] = jnp.concatenate(tail, 1)
+            g.send_lat[level, end] = bf(stage[...])
+            for og in range(2):
+                main = ext[level, 1 + og, lo : lo + 40, 0:128]
+                tail = [ext[level, 1 + og, lo + n : lo + n + 24, 128:192] for n in (0, 18)]
+                g.send_corner[level, 2 * end + og] = bf(jnp.concatenate([main, jnp.concatenate(tail, 1)], 0))
 
     def send_level(level):
         lon_s, lat_s, cor_s = g.send_lon, g.send_lat, g.send_corner
@@ -266,13 +269,14 @@
                 y = g.recv_corner[level, 2 * end + side].astype(jnp.float32)
                 lo = 5 * LIVE * end
                 ext[level, c, lo : lo + LIVE, 0:128] = y[0:LIVE]
-                ext[level, c, lo : lo + LIVE, 128:192] = y[40 : 40 + LIVE, 0:64]
+                for n in range(2):
+                    ext[level, c, lo + 18 * n : lo + 18 * n + 18, 128:192] = y[40:58, 64 * n : 64 * n + 64]
         for end in range(2):
             x = g.recv_lat[level, end].astype(jnp.float32)
             lo = 5 * LIVE * end
             for og in range(2):
-                ext[level, 1 + og, lo : lo + LIVE, 0:128] = x[og * 40 : og * 40 + LIVE]
-                ext[level, 1 + og, lo : lo + LIVE, 128:192] = x[80 : 80 + LIVE, og * 64 : og * 64 + 64]
+                ext[level, 1 + og, lo : lo + LIVE, 0:128] = x[og * LIVE : og * LIVE + LIVE]
+                ext[level, 1 + og, lo : lo + LIVE, 128:192] = x[72:108, og * 64 : og * 64 + 64]
 
     pack_level(0)
     pl.semaphore_wait(barrier, 10)
@@ -291,10 +295,28 @@
         start(ids.at[0], ids.at[4], at(0, 2)),
         start(ids.at[0], ids.at[5], at(1, 2)),
     ]
-    table_copy_one = start(v.table_one.at[1], g.table_in_one, at(1, 0))
+    def pack_table(table, which, heads, packed):
+        packed[...] = jnp.zeros_like(packed)
+        for n, lane in enumerate(LATER):
+            wide = min(512, PAIRS - lane)
+            packed[n, :, :, 0:wide] = table[which, pl.ds(heads * odd, heads), :, lane : lane + wide]
+
+    def unpack_table(flat, tables, heads):
+        for half in range(2):
+            for n, lane in enumerate(LATER):
+                for h in range(heads):
+                    row = 2 * (half * heads + h)
+                    flat[0, row : row + 2, lane : lane + 512] = tables[half, n, h].astype(jnp.float32)
+
+    def to_other_core(tables):
+        return start(tables.at[odd], tables.at[odd], at(0, 1 - 2 * odd))
+
+    pack_table(v.table_one, 1, H1 // 2, g.table_out_one)
+    table_copy_one = start(g.table_out_one, g.table_in_one.at[odd], at(1, 0))
     pack_level(1)
     first.append(send_level(1))
-    table_copy_two = start(v.table_two.at[0], g.table_in_two, at(1, 0))
+    pack_table(v.table_two, 0, H2 // 2, g.table_out_two)
+    table_copy_two = start(g.table_out_two, g.table_in_two.at[odd], at(1, 0))
 
     lane_one = lax.broadcasted_iota(jnp.int32, (D1, 256), 1)
     weight = v.project_one[...].astype(jnp.float32)
@@ -358,9 +380,7 @@
         flat_two[1, 2 * h : 2 * h + 2, 0:PAIRS] = v.table_two[0, h].astype(jnp.float32)
     fill_two(1)
     table_copy_one.wait_recv()
-    for h in range(H1):
-        flat_one[0, 2 * h : 2 * h + 2, 0:PAIRS] = g.table_in_one[h].astype(jnp.float32)
-    fill_one(0)
+    table_copy_one = to_other_core(g.table_in_one)
 
     for copy in id_copies:
         copy.wait_recv()
@@ -398,6 +418,10 @@
             same = jnp.where(number + FEATURE == lane_number, 1.0, 0.0)
             g.key_mask_two[level, oh] = same + (1.0 - alive_two) * table[6 + oh]
             g.query_mask_two[level, oh] = (table[8 + oh] - same) * (-FAR)
+
+    table_copy_one.wait_recv()
+    unpack_table(flat_one, g.table_in_one, H1 // 2)
+    fill_one(0)
 
     queries, heads = g.queries, g.heads
 
@@ -438,7 +462,8 @@
         inner = dot(normed, v.up[...])
         inner = bf(0.5 * inner * (1.0 + lax.erf(inner * 0.5**0.5)))
         block = bf(state.astype(jnp.float32) + dot_t(inner, v.down[...]))
-        parts = [dot(v.merge[n * 72 : n * 72 + 72], block) for n in range(4)]
+        parts = dot(v.merge[...], block)
+        parts = [parts[n * 72 : n * 72 + 72] for n in range(4)]
         center = sum(jnp.sum(p, -1, keepdims=True) for p in parts) / (4 * D1)
         parts = [p - center for p in parts]
         scale = lax.rsqrt(sum(jnp.sum(p * p, -1, keepdims=True) for p in parts) / (4 * D1) + 1e-5)
@@ -508,13 +533,14 @@
     second = [section_one(0)]
     own_queries(0)
     wait_all(first[1])
+    table_copy_two.wait_recv()
+    table_copy_two = to_other_core(g.table_in_two)
     unpack_level(1)
     second.append(section_one(1))
     own_queries(1)
 
     table_copy_two.wait_recv()
-    for h in range(H2):
-        flat_two[0, 2 * h : 2 * h + 2, 0:PAIRS] = g.table_in_two[h].astype(jnp.float32)
+    unpack_table(flat_two, g.table_in_two, H2 // 2)
     fill_two(0)
 
     wait_all(second[0])
@@ -600,18 +626,21 @@
         rows_in=vmem((12, 12, 8, D1), f32),
         send_lon=vmem((2, 2, 224, 128), b16),
         recv_lon=vmem((2, 2, 224, 128), b16),
-        send_lat=vmem((2, 2, 128, 128), b16),
-        recv_lat=vmem((2, 2, 128, 128), b16),
-        send_corner=vmem((2, 4, 80, 128), b16),
-        recv_corner=vmem((2, 4, 80, 128), b16),
+        stage=vmem((112, 128), f32),
+        send_lat=vmem((2, 2, 112, 128), b16),
+        recv_lat=vmem((2, 2, 112, 128), b16),
+        send_corner=vmem((2, 4, 64, 128), b16),
+        recv_corner=vmem((2, 4, 64, 128), b16),
         send_all=vmem((2, 80, D2), b16),
         recv_all=vmem((2, 80, D2), b16),
         send_end=vmem((2, 2, 48, D2), b16),
         recv_end=vmem((2, 2, 2, 48, D2), b16),
         ids=vmem((6, 16, 128), b16),
         region=vmem((12, 8, 128), f32),
-        table_in_one=vmem((H1, 2, PAIRS), b16),
-        table_in_two=vmem((H2, 2, PAIRS), b16),
+        table_out_one=vmem((4, H1 // 2, 2, 512), b16),
+        table_out_two=vmem((4, H2 // 2, 2, 512), b16),
+        table_in_one=vmem((2, 4, H1 // 2, 2, 512), b16),
+        table_in_two=vmem((2, 4, H2 // 2, 2, 512), b16),
         flat_one=vmem((3, 16, TABLE), f32),
         flat_two=vmem((2, 24, TABLE), f32),
         left_one=vmem((8, 216, 512), f32),
@@ -637,8 +666,8 @@
     )
     held = [vmem(x.shape, x.dtype) for x in fetched.values()]
     sems = dict(
-        send=pltpu.SemaphoreType.DMA((33,)),
-        recv=pltpu.SemaphoreType.DMA((33,)),
+        send=pltpu.SemaphoreType.DMA((35,)),
+        recv=pltpu.SemaphoreType.DMA((35,)),
         load=pltpu.SemaphoreType.DMA((len(fetched),)),
     )
     spec = lambda name: pl.BlockSpec(memory_space=pl.ANY if name in fetched else vmem)

time: 46.5 us -> 44.7 us (0.961)
  Pallas kernels: 44.7 us -> 43 us
    pallas_call x1, Pallas kernels: 44.7 us -> 43 us  [shards(): pl.pallas_call(functools.partial(kernel, lat_size, lon_size, names, tuple...]
where the time goes in v3:
time: 44.7 us; the launch traced here: 44.6 us
  Pallas kernels  43 us (96%)
  local copies, waits for them, and re-layouts  1.58 us (4%)
    pallas_call x1, Pallas kernels, shards(): pl.pallas_call(functools.partial(kernel, lat_size, lon_size, names, tuple...  43 us
    unnamed x1, local copies, waits for them, and re-layouts  1.58 us

profile of v3, /device:TPU:1, one launch (start us, length us, event | category | flops | bytes accessed | tf_op | source)
XLA Modules:
  0.0 44.6 jit_solution(9237143243957712613)
XLA Ops:
  0.0 43.0 %block.1 = bf16[6,6,4,384]{3,2,1,0:T(4,128)(2,1)} custom-call(s32[1,96]{1,0:T(1,128)} %bitcast.19, f32[1,192]{1,0:T(1,128)} %bitcast.17, f32[1,192]{1,0:T(1,128)} %bitcast.18, f32[768]{0:T(1024)} %refs_3_.1, f32[384]{0:T(512)} %refs_4_.1, bf16[12,12,4,192]{3,2,1,0:T(4,128)(2,1)} %bitcast.11, bf16[160,288]{1,0:T(8,128)(2,1)} %constant.40.clone.refs_6_, ...), custom_call_target="tpu_custom_call" | custom-call | tf_op jit(solution)/shard_map/block/pallas_call | solution.py:675
  43.0 1.6 %copy.39 = bf16[4,6,6,384]{3,0,2,1:T(4,128)(2,1)} copy(bf16[4,6,6,384]{3,0,2,1:T(4,128)(2,1)} %bitcast.10) | data formatting | bytes 221184

commit v4 on v3

--- a/solution.py
+++ b/solution.py
@@ -248,10 +248,10 @@
         lon_s, lat_s, cor_s = g.send_lon, g.send_lat, g.send_corner
         lon_r, lat_r, cor_r = g.recv_lon, g.recv_lat, g.recv_corner
         return [
+            start(lat_s.at[level, 0], lat_r.at[level, 1], at(-1, 0)),
+            start(lat_s.at[level, 1], lat_r.at[level, 0], at(1, 0)),
             start(lon_s.at[level, 0], lon_r.at[level, 1], at(0, -1)),
             start(lon_s.at[level, 1], lon_r.at[level, 0], at(0, 1)),
-            start(lat_s.at[level, 0], lat_r.at[level, 1], at(-1, 0)),
-            start(lat_s.at[level, 1], lat_r.at[level, 0], at(1, 0)),
             start(cor_s.at[level, 0], cor_r.at[level, 3], at(-1, -1)),
             start(cor_s.at[level, 1], cor_r.at[level, 2], at(-1, 1)),
             start(cor_s.at[level, 2], cor_r.at[level, 1], at(1, -1)),
@@ -482,11 +482,11 @@
         to = 2 * odd - 1
         ends, into = g.send_end, g.recv_end
         return [
-            start(g.send_all.at[level], g.recv_all.at[level], at(0, to)),
             start(ends.at[level, 0], into.at[level, 0, 1], at(-1, 0)),
             start(ends.at[level, 1], into.at[level, 0, 0], at(1, 0)),
             start(ends.at[level, 0], into.at[level, 1, 1], at(-1, to)),
             start(ends.at[level, 1], into.at[level, 1, 0], at(1, to)),
+            start(g.send_all.at[level], g.recv_all.at[level], at(0, to)),
         ]
 
     def own_queries(level):

time: 44.7 us -> 44.7 us (level)
  no operation moved by 1% of the time
where the time goes in v4:
time: 44.7 us; the launch traced here: 44.6 us
  Pallas kernels  43 us (96%)
  local copies, waits for them, and re-layouts  1.58 us (4%)
    pallas_call x1, Pallas kernels, shards(): pl.pallas_call(functools.partial(kernel, lat_size, lon_size, names, tuple...  43 us
    unnamed x1, local copies, waits for them, and re-layouts  1.58 us

profile of v4, /device:TPU:1, one launch (start us, length us, event | category | flops | bytes accessed | tf_op | source)
XLA Modules:
  0.0 44.6 jit_solution(10739159270717655196)
XLA Ops:
  0.0 43.0 %block.1 = bf16[6,6,4,384]{3,2,1,0:T(4,128)(2,1)} custom-call(s32[1,96]{1,0:T(1,128)} %bitcast.19, f32[1,192]{1,0:T(1,128)} %bitcast.17, f32[1,192]{1,0:T(1,128)} %bitcast.18, f32[768]{0:T(1024)} %refs_3_.1, f32[384]{0:T(512)} %refs_4_.1, bf16[12,12,4,192]{3,2,1,0:T(4,128)(2,1)} %bitcast.11, bf16[160,288]{1,0:T(8,128)(2,1)} %constant.40.clone.refs_6_, ...), custom_call_target="tpu_custom_call" | custom-call | tf_op jit(solution)/shard_map/block/pallas_call | solution.py:675
  43.0 1.6 %copy.39 = bf16[4,6,6,384]{3,0,2,1:T(4,128)(2,1)} copy(bf16[4,6,6,384]{3,0,2,1:T(4,128)(2,1)} %bitcast.10) | data formatting | bytes 221184

commit v5 on v3

--- a/solution.py
+++ b/solution.py
@@ -354,15 +354,19 @@
     flat_one[...] = jnp.zeros_like(flat_one)
     flat_two[...] = jnp.zeros_like(flat_two)
 
+    def expand_one(block):
+        left = bf(left_one[block])
+        for og in range(2):
+            bias_one[block, og] = dot_t(v.shift[1 - og], left)
+
     def fill_one(ag):
         window, first_row = ((0, 3), (1, 0), (1, 3), (2, 0))[ag]
         part = dot(v.choose_one[...], window_rows(flat_one, window, first_row))
         for level in range(2):
             block = level * 4 + ag
             shifted(left_one, block, part[level * 36 : level * 36 + 36])
-            left = bf(left_one[block])
-            for og in range(2):
-                bias_one[block, og] = dot_t(v.shift[1 - og], left)
+            if level == 0:
+                expand_one(block)
 
     def fill_two(ag):
         part = dot(v.choose_two[...], window_rows(flat_two, ag, 3 - 3 * ag))
@@ -532,6 +536,8 @@
     unpack_level(0)
     second = [section_one(0)]
     own_queries(0)
+    for block in range(4, 8):
+        expand_one(block)
     wait_all(first[1])
     table_copy_two.wait_recv()
     table_copy_two = to_other_core(g.table_in_two)

time: 44.7 us -> 45 us (level)
  no operation moved by 1% of the time
where the time goes in v5:
time: 45 us; the launch traced here: 44.8 us
  Pallas kernels  43.2 us (96%)
  local copies, waits for them, and re-layouts  1.58 us (4%)
    pallas_call x1, Pallas kernels, shards(): pl.pallas_call(functools.partial(kernel, lat_size, lon_size, names, tuple...  43.2 us
    unnamed x1, local copies, waits for them, and re-layouts  1.58 us

profile of v5, /device:TPU:1, one launch (start us, length us, event | category | flops | bytes accessed | tf_op | source)
XLA Modules:
  0.0 44.8 jit_solution(14261285582898622226)
XLA Ops:
  0.0 43.2 %block.1 = bf16[6,6,4,384]{3,2,1,0:T(4,128)(2,1)} custom-call(s32[1,96]{1,0:T(1,128)} %bitcast.19, f32[1,192]{1,0:T(1,128)} %bitcast.17, f32[1,192]{1,0:T(1,128)} %bitcast.18, f32[768]{0:T(1024)} %refs_3_.1, f32[384]{0:T(512)} %refs_4_.1, bf16[12,12,4,192]{3,2,1,0:T(4,128)(2,1)} %bitcast.11, bf16[160,288]{1,0:T(8,128)(2,1)} %constant.40.clone.refs_6_, ...), custom_call_target="tpu_custom_call" | custom-call | tf_op jit(solution)/shard_map/block/pallas_call | solution.py:681
  43.2 1.6 %copy.39 = bf16[4,6,6,384]{3,0,2,1:T(4,128)(2,1)} copy(bf16[4,6,6,384]{3,0,2,1:T(4,128)(2,1)} %bitcast.10) | data formatting | bytes 221184
